TPU v7x, 128 devices: a whole 4x4x4 slice. The times are simulated.
128 devices in a mesh: gx: 8 (over z, core), gy: 16 (over x, y).
Axes of the slice: x: 4, y: 4, z: 4, core: 2. Of those that a mesh axis runs over, the one named last changes fastest.
Arguments:
- compressed: bfloat16 [128, 1536], P(None, 'gx'), may hold values from -6 to 6
- query_up: bfloat16 [1536, 24576], P('gx', 'gy'), may hold values from -0.15625 to 0.15625
- key_absorb: bfloat16 [128, 128, 512], P('gy'), may hold values from -1 to 1
- value_up: bfloat16 [128, 512, 128], P('gy'), may hold values from -0.25 to 0.25
- out_proj: bfloat16 [16384, 7168], P('gy', 'gx'), may hold values from -0.046875 to 0.046875
- cache_latent: bfloat16 [128, 16384, 512], P(('gx', 'gy')), may hold values from -6 to 6
- cache_rope: bfloat16 [128, 64, 16384], P(('gx', 'gy')), may hold values from -6 to 6
- lengths: int32 [128], replicated, may hold values from 1 to 16384, as said below
- holder: int32 [128], replicated, may hold values from 0 to 127, each once
Outputs:
- attended: bfloat16 [128, 7168], P('gy', 'gx')
Inputs may be any that keep to these rules, and one draw needn't show every extreme that they name: `lengths`: some request has exactly 16384 valid positions.
All inputs are finite; a program needn't handle non-finite values.
Results may differ from a plain program's by a relative error of at most 0.02.
Values may be sent and summed in bfloat16 or wider, within the bound.
No kernel may reach another device: no remote copies, remote signals or barrier semaphores. Data moves between devices by JAX's collectives and lax.ppermute only.
A program may use at most 128 MiB of HBM per device.

v0:
```python
import math

import jax
import jax.numpy as jnp
from jax import lax
from jax.sharding import PartitionSpec as P

KVL = 512
ROPE = 64
NOPE = 128
VH = 128


def rotate(halves, positions):
    half_width = halves.shape[-1] // 2
    frequency = 10000.0 ** (-2.0 * jnp.arange(half_width).astype(jnp.float32) / halves.shape[-1])
    angles = positions.astype(jnp.float32)[:, None, None] * frequency
    former = halves[..., :half_width]
    latter = halves[..., half_width:]
    return jnp.concatenate(
        [
            former * jnp.cos(angles) - latter * jnp.sin(angles),
            former * jnp.sin(angles) + latter * jnp.cos(angles),
        ],
        axis=-1,
    )


def attend(query_lat, query_rope, latent, rope_keys, length):
    scores = lax.dot_general(
        query_lat, latent, (((1,), (1,)), ((), ())), preferred_element_type=jnp.float32
    )
    scores = scores + jnp.dot(query_rope, rope_keys, preferred_element_type=jnp.float32)
    scores = scores * (1.0 / math.sqrt(NOPE + ROPE))
    places = jnp.arange(latent.shape[0])
    scores = jnp.where(places[None, :] < length, scores, -1e30)
    largest = jnp.max(scores, axis=1, keepdims=True)
    expos = jnp.exp(scores - largest)
    weights = (expos / jnp.sum(expos, axis=1, keepdims=True)).astype(jnp.bfloat16)
    return jnp.dot(weights, latent, preferred_element_type=jnp.float32).astype(jnp.bfloat16)


def local(
    compressed, query_up, key_absorb, value_up, out_proj, cache_latent, cache_rope, lengths, holder
):
    count_gx = lax.axis_size("gx")
    count_gy = lax.axis_size("gy")
    index_gx = lax.axis_index("gx")
    index_gy = lax.axis_index("gy")
    batch = compressed.shape[0]
    local_heads = key_absorb.shape[0]
    own_heads = local_heads // count_gx
    partial_sum = jnp.dot(compressed, query_up, preferred_element_type=jnp.float32)
    projected = lax.psum_scatter(partial_sum, "gx", scatter_dimension=1, tiled=True)
    projected = projected.reshape(batch, own_heads, NOPE + ROPE)
    nope_part = projected[..., :NOPE].astype(jnp.bfloat16)
    rope_part = rotate(projected[..., NOPE:], lengths - 1).astype(jnp.bfloat16)
    absorb_own = lax.dynamic_slice_in_dim(key_absorb, index_gx * own_heads, own_heads, 0)
    absorbed = jnp.einsum(
        "bhn,hnc->bhc", nope_part, absorb_own, preferred_element_type=jnp.float32
    ).astype(jnp.bfloat16)
    selector = (holder[:, None] == jnp.arange(batch, dtype=jnp.int32)[None, :]).astype(jnp.bfloat16)
    send_lat = jnp.einsum(
        "dr,rhc->dhc", selector, absorbed, preferred_element_type=jnp.float32
    ).astype(jnp.bfloat16)
    send_rope = jnp.einsum(
        "dr,rhc->dhc", selector, rope_part, preferred_element_type=jnp.float32
    ).astype(jnp.bfloat16)
    got_lat, got_rope = (
        lax.all_to_all(send_lat, ("gx", "gy"), split_axis=0, concat_axis=1, tiled=True),
        lax.all_to_all(send_rope, ("gx", "gy"), split_axis=0, concat_axis=1, tiled=True),
    )
    query_lat = got_lat.reshape(-1, KVL)
    query_rope = got_rope.reshape(-1, ROPE)
    slot_index = index_gx * count_gy + index_gy
    request = holder[slot_index]
    length = lengths[request]
    latent_out = attend(query_lat, query_rope, cache_latent[0], cache_rope[0], length)
    send_back = latent_out.reshape(-1, 1, KVL)
    returned = lax.all_to_all(send_back, ("gx", "gy"), split_axis=0, concat_axis=1, tiled=True)
    by_request = jnp.einsum(
        "dr,hdc->rhc", selector, returned, preferred_element_type=jnp.float32
    ).astype(jnp.bfloat16)
    value_own = lax.dynamic_slice_in_dim(value_up, index_gx * own_heads, own_heads, 0)
    head_values = jnp.einsum(
        "rhc,hcv->rhv", by_request, value_own, preferred_element_type=jnp.float32
    ).astype(jnp.bfloat16)
    head_values = head_values.reshape(batch, own_heads * VH)
    all_values = lax.all_gather(head_values, "gx", axis=1, tiled=True)
    return lax.psum_scatter(
        jnp.dot(all_values, out_proj, preferred_element_type=jnp.float32).astype(jnp.bfloat16),
        "gy",
        scatter_dimension=0,
        tiled=True,
    )


def solution(mesh):
    in_specs = (
        P(None, "gx"),
        P("gx", "gy"),
        P("gy", None, None),
        P("gy", None, None),
        P("gy", "gx"),
        P(("gx", "gy"), None, None),
        P(("gx", "gy"), None, None),
        P(),
        P(),
    )
    out_specs = P("gy", "gx")
    return jax.shard_map(local, mesh=mesh, in_specs=in_specs, out_specs=out_specs, check_vma=False)
```

profile of v0, /device:TPU:0, one launch (start us, length us, event | category | flops | bytes accessed | tf_op | source)
XLA Modules:
  0.0 227.7 jit_solution(2425595912014590506)
XLA Ops:
  6.5 2.6 %fusion.61 = f32[128,1536]{0,1:T(8,128)} fusion(bf16[128,192]{0,1:T(8,128)(2,1)} %param.9, bf16[192,1536]{1,0:T(8,128)(2,1)} %param.10), kind=kOutput, calls=%fused_computation.65 | convolution fusion | flops 75497472 | bytes 1425408 | tf_op jit(solution)/shard_map/dot_general | solution.py:53
  9.1 1.2 dynamic_slice.13
  12.3 1.2 dynamic_slice.14
  13.6 0.7 add_convert_fusion
  14.2 29.6 %reduce-scatter.2.cloned.1.call-done = f32[128,192]{0,1:T(8,128)} async-done(((f32[128,1536]{0,1:T(8,128)}), f32[128,192]{0,1:T(8,128)}) %reduce-scatter.2.cloned.1.call-update) | async-done | bytes 98320 | tf_op jit(solution)/shard_map/reduce_scatter | solution.py:54
  43.8 0.9 fusion.55
  44.7 0.9 fusion.21
  45.5 0.8 copy.14
  46.3 7.4 %all-to-all-start.1 = ((bf16[128,1,64]{2,1,0:T(2,128)(2,1)}), bf16[128,1,64]{2,1,0:T(2,128)(2,1)S(1)}, u32[]{:S(2)}, u32[]{:S(2)}) async-start(bf16[128,1,64]{2,1,0:T(2,128)(2,1)} %copy.14), calls=%async_computation.2 | async-start | bytes 131072 | tf_op jit(solution)/shard_map/all_to_all | solution.py:71
  53.7 1.3 fusion.14
  55.1 0.5 broadcast.82
  55.6 0.7 reduce
  56.3 0.7 reshape.182
  56.9 6.3 %all-to-all-done.1 = bf16[128,1,64]{2,1,0:T(2,128)(2,1)S(1)} async-done(((bf16[128,1,64]{2,1,0:T(2,128)(2,1)}), bf16[128,1,64]{2,1,0:T(2,128)(2,1)S(1)}, u32[]{:S(2)}, u32[]{:S(2)}) %all-to-all-start.1) | async-done | bytes 16416 | tf_op jit(solution)/shard_map/all_to_all | solution.py:71
  63.2 4.6 %all-to-all-start = ((bf16[128,2,256]{2,1,0:T(2,128)(2,1)}), bf16[128,2,256]{2,1,0:T(2,128)(2,1)S(1)}, u32[]{:S(2)}, u32[]{:S(2)}) async-start(bf16[128,2,256]{2,1,0:T(2,128)(2,1)} %reshape.182), calls=%async_computation.1 | async-start | bytes 262144 | tf_op jit(solution)/shard_map/all_to_all | solution.py:70
  67.9 0.6 iota_compare_fusion
  68.5 0.1 copy.15
  68.6 8.9 %all-to-all-done = bf16[128,2,256]{2,1,0:T(2,128)(2,1)S(1)} async-done(((bf16[128,2,256]{2,1,0:T(2,128)(2,1)}), bf16[128,2,256]{2,1,0:T(2,128)(2,1)S(1)}, u32[]{:S(2)}, u32[]{:S(2)}) %all-to-all-start) | async-done | bytes 131104 | tf_op jit(solution)/shard_map/all_to_all | solution.py:70
  77.4 0.1 reshape.183
  77.5 14.5 %fusion.4 = f32[128,16384]{1,0:T(8,128)} fusion(bf16[1,16384,512]{2,1,0:T(8,128)(2,1)} %param.14, bf16[128,1,512]{2,1,0:T(2,128)(2,1)S(1)} %reshape.183), kind=kOutput, calls=%fused_computation.5 | convolution fusion | flops 2147483648 | bytes 25296896 | tf_op jit(solution)/shard_map/dot_general | solution.py:30
  92.0 5.2 %fusion.60 = (f32[128]{0:T(128)S(1)}, f32[128,16384]{1,0:T(8,128)S(1)}) fusion(f32[128,16384]{1,0:T(8,128)} %fusion.4, bf16[1,64,16384]{2,1,0:T(8,128)(2,1)S(1)} %copy-done, bf16[128,1,64]{0,2,1:T(8,128)(2,1)S(1)} %copy.15, pred[16384]{0:T(1024)(128)(4,1)S(1)} %iota_compare_fusion), kind=kOutput, calls=%fused_computation.64 | convolution fusion | flops 276823936 | bytes 18907648 | tf_op jit(solution)/shard_map/dot_general | solution.py:33
  97.2 1.6 fusion.6
  98.8 8.8 %fusion.15 = bf16[128,1,512]{2,0,1:T(8,128)(2,1)S(1)} fusion(bf16[1,16384,512]{2,1,0:T(8,128)(2,1)} %param.14, f32[128,16384]{1,0:T(8,128)S(1)} %get-tuple-element.8, f32[128]{0:T(128)S(1)} %fusion.6, f32[128]{0:T(128)S(1)} %get-tuple-element.7), kind=kOutput, calls=%fused_computation.20 | convolution fusion | flops 2153840640 | bytes 25297920 | tf_op jit(solution)/shard_map/dot_general | solution.py:40
  107.6 0.7 reduce.1
  108.3 14.2 %all_to_all.12 = bf16[128,2,256]{2,1,0:T(2,128)(2,1)S(1)} all-to-all(bf16[128,2,256]{2,1,0:T(2,128)(2,1)S(1)} %reshape.184), channel_id=1, replica_groups=mesh['gx'=8,'gy'=16] {'gx','gy'}, dimensions={0} | all-to-all | bytes 262144 | tf_op jit(solution)/shard_map/all_to_all | solution.py:80
  122.5 0.1 reshape.185
  122.6 1.4 fusion.20
  124.0 12.8 %all-gather = bf16[128,1,1024]{0,2,1:T(8,128)(2,1)S(1)} all-gather(bf16[128,1,128]{0,2,1:T(8,128)(2,1)S(1)} %fusion.20), channel_id=2, replica_groups=mesh['gx'=8,'gy'=16] {'gx'}, dimensions={2}, use_global_device_ids=true | all-gather | bytes 294912 | tf_op jit(solution)/shard_map/all_gather | solution.py:89
  136.8 2.7 %convolution_convert_fusion = bf16[128,896]{1,0:T(8,128)(2,1)} fusion(bf16[1024,896]{1,0:T(8,128)(2,1)} %param.13, bf16[128,1,1024]{0,2,1:T(8,128)(2,1)S(1)} %all-gather), kind=kOutput, calls=%fused_computation.13 | convolution fusion | flops 234995712 | bytes 2326528 | tf_op jit(solution)/shard_map/dot_general | solution.py:91
  139.5 0.6 dynamic-slice
  140.8 78.8 %all-reduce.3.cloned.1.call-done = bf16[128,896]{1,0:T(8,128)(2,1)} async-done(((bf16[128,896]{1,0:T(8,128)(2,1)}), bf16[128,896]{1,0:T(8,128)(2,1)}) %all-reduce.3.cloned.1.call-update) | async-done | bytes 229392
  219.6 1.3 constant_dynamic-slice_fusion
  (12 shorter events, 0.1 us)
Async XLA Ops:
  6.5 85.5 %copy-start = (bf16[1,64,16384]{2,1,0:T(8,128)(2,1)S(1)}, bf16[1,64,16384]{2,1,0:T(8,128)(2,1)}, u32[]{:S(2)}) copy-start(bf16[1,64,16384]{2,1,0:T(8,128)(2,1)} %param.15) | copy-start | bytes 6291460
  6.5 37.3 %reduce-scatter.2.cloned.1.call-start = ((), (), s32[]{:S(2)}) async-start(), calls=%async_computation.4 | async-start | bytes 884736 | tf_op jit(solution)/shard_map/reduce_scatter | solution.py:54
  46.3 16.9 %all-to-all-start.1 = ((bf16[128,1,64]{2,1,0:T(2,128)(2,1)}), bf16[128,1,64]{2,1,0:T(2,128)(2,1)S(1)}, u32[]{:S(2)}, u32[]{:S(2)}) async-start(bf16[128,1,64]{2,1,0:T(2,128)(2,1)} %copy.14), calls=%async_computation.2 | async-start | bytes 131072 | tf_op jit(solution)/shard_map/all_to_all | solution.py:71
  63.2 14.2 %all-to-all-start = ((bf16[128,2,256]{2,1,0:T(2,128)(2,1)}), bf16[128,2,256]{2,1,0:T(2,128)(2,1)S(1)}, u32[]{:S(2)}, u32[]{:S(2)}) async-start(bf16[128,2,256]{2,1,0:T(2,128)(2,1)} %reshape.182), calls=%async_computation.1 | async-start | bytes 262144 | tf_op jit(solution)/shard_map/all_to_all | solution.py:70
  67.8 151.7 %all-reduce.3.cloned.1.call-start = ((), (), s32[]{:S(2)}) async-start(), calls=%async_computation.5 | async-start | bytes 458752
  98.7 23.9 %copy-start.1 = (s32[128]{0:T(128)S(1)}, s32[128]{0:T(128)}, u32[]{:S(2)}) copy-start(s32[128]{0:T(128)} %param.17) | copy-start | bytes 1540
  98.8 40.8 %copy-start.2 = (u32[128]{0:T(128)S(1)}, u32[128]{0:T(128)}, u32[]{:S(2)}) copy-start(u32[128]{0:T(128)} %constant.41) | copy-start | bytes 1540
Sparse Core Ops, SparseCore 0:
  9.7 34.0 reduce-scatter.1
  139.7 79.8 all-reduce.2
where the time goes:
time: 228 us
  waiting for transfers between devices  124 us (54%)
  matrix products  37.2 us (16%)
  blocking collectives  27.1 us (12%)
  between operations  16.1 us (7%)
  starting transfers between devices  12.1 us (5%)
  local copies, waits for them, and re-layouts  6.67 us (3%)
  other arithmetic  5.03 us (2%)
    unnamed x3, waiting for transfers between devices  78.8 us
    reduce_scatter x1, waiting for transfers between devices, local(): lax.psum_scatter(partial_sum, 'gx', scatter_dimension=1, tiled=True)  29.6 us
    dot_general x1, matrix products, attend(): lax.dot_general(query_lat, latent, (((1,), (1,)), ((), ())), preferred_el...  14.5 us
    all_to_all x1, blocking collectives, local(): lax.all_to_all(send_back, ('gx', 'gy'), split_axis=0, concat_axis=1, tile...  14.2 us
    all_gather x1, blocking collectives, local(): all_values = lax.all_gather(head_values, 'gx', axis=1, tiled=True)  12.8 us
    all_to_all x1, waiting for transfers between devices, local(): lax.all_to_all(send_lat, ('gx', 'gy'), split_axis=0, concat_axis=1, tiled...  8.88 us
    dot_general x1, matrix products, attend(): jnp.dot(weights, latent, preferred_element_type=jnp.float32)  8.81 us
    all_to_all x1, starting transfers between devices, local(): lax.all_to_all(send_rope, ('gx', 'gy'), split_axis=0, concat_axis=1, tile...  7.42 us
  transfers between devices with their start and end apart: 4, of which 4 were waited for; matrix products, arithmetic and copies ran while one was open for 3% of the time, Pallas kernels for 0%

commit v1 on v0

v1 whole, which is shorter than its diff:
```python
import math

import jax
import jax.numpy as jnp
from jax import lax
from jax.experimental import pallas as pl
from jax.experimental.pallas import tpu as pltpu
from jax.sharding import PartitionSpec as P

KVL = 512
ROPE = 64
NOPE = 128
HEAD = NOPE + ROPE
VH = 128
WIDE = 640
CHUNK = 4096
PIECE = 2048
VMEM = pl.BlockSpec(memory_space=pltpu.VMEM)
SMEM = pl.BlockSpec(memory_space=pltpu.SMEM)
ANY = pl.BlockSpec(memory_space=pl.ANY)
F32 = jnp.float32
BF16 = jnp.bfloat16


def dot(a, b, contract_a=1, contract_b=0):
    return lax.dot_general(
        a, b, (((contract_a,), (contract_b,)), ((), ())), preferred_element_type=F32
    )


def holder_matrix(holder_row):
    count = holder_row.shape[1]
    requests = lax.broadcasted_iota(jnp.int32, (count, count), 0)
    return (requests == holder_row).astype(F32).astype(BF16)


def project_kernel(holder_ref, compressed_ref, query_up_ref, mine_ref, other_ref, part_ref):
    core = lax.rem(lax.axis_index("gx"), 2)
    by_slot = dot(compressed_ref[...], holder_matrix(holder_ref[...])).astype(BF16)
    part_ref[...] = dot(by_slot, query_up_ref[...], 0, 0)
    for z in range(4):
        mine_ref[z * 16 : z * 16 + 16, :] = part_ref[pl.ds(z * 32 + core * 16, 16), :]
        other_ref[z * 16 : z * 16 + 16, :] = part_ref[pl.ds(z * 32 + 16 - core * 16, 16), :].astype(
            BF16
        )


def pair_kernel(mine_ref, got_ref, own_ref, one_ref, two_ref, three_ref):
    z = lax.div(lax.axis_index("gx"), 2)
    for k, out_ref in enumerate((own_ref, one_ref, two_ref, three_ref)):
        rows = pl.ds(pl.multiple_of((z ^ k) * 16, 16), 16)
        out_ref[...] = (mine_ref[rows, :] + got_ref[rows, :].astype(F32)).astype(out_ref.dtype)


def absorb_kernel(
    own_ref, one_ref, two_ref, three_ref, keep_ref, minus_ref, plus_ref, absorb_ref, out_ref, wide_ref
):
    queries = (
        own_ref[...]
        + one_ref[...].astype(F32)
        + two_ref[...].astype(F32)
        + three_ref[...].astype(F32)
    )
    width = queries.shape[1]
    half = ROPE // 2
    queries = (
        queries * keep_ref[...]
        + pltpu.roll(queries, width - half, 1) * minus_ref[...]
        + pltpu.roll(queries, half, 1) * plus_ref[...]
    )
    shifted = pltpu.roll(queries, width - 64, 1)
    blank = jnp.zeros((queries.shape[0], WIDE - KVL - ROPE), F32)
    for h in range(absorb_ref.shape[0]):
        start = h * HEAD
        source = queries if start % 128 == 0 else shifted
        start -= start % 128
        nope = source[:, start : start + NOPE].astype(BF16)
        start = h * HEAD + NOPE
        source = queries if start % 128 == 0 else shifted
        start -= start % 128
        rope = source[:, start : start + ROPE]
        wide_ref[:, h, :KVL] = dot(nope, absorb_ref[h])
        wide_ref[:, h, KVL:] = jnp.concatenate([rope, blank], axis=1)
    out_ref[...] = wide_ref[...].reshape(out_ref.shape).astype(BF16)


def attend_kernel(
    length_ref, query_ref, latent_hbm, rope_hbm, out_ref, latent, rope, scores, top, total, acc, sems
):
    length = length_ref[0]
    places = latent.shape[0]
    scale = math.log2(math.e) / math.sqrt(HEAD)

    def copies(i):
        at = pl.ds(i * PIECE, PIECE)
        return (
            pltpu.make_async_copy(latent_hbm.at[0, at, :], latent.at[at, :], sems.at[0, i]),
            pltpu.make_async_copy(rope_hbm.at[0, :, at], rope.at[:, at], sems.at[1, i]),
        )

    for i in range(places // PIECE):

        @pl.when(i * PIECE < length)
        def _():
            for copy in copies(i):
                copy.start()

    top[...] = jnp.full(top.shape, -1e30, F32)
    total[...] = jnp.zeros(total.shape, F32)
    acc[...] = jnp.zeros(acc.shape, F32)
    query_lat = query_ref[:, :KVL]
    query_rope = query_ref[:, KVL : KVL + ROPE]
    per = CHUNK // PIECE
    for c in range(places // CHUNK):
        at = pl.ds(c * CHUNK, CHUNK)

        @pl.when(c * CHUNK < length)
        def _():
            for i in range(c * per, c * per + per):

                @pl.when(i * PIECE < length)
                def _():
                    for copy in copies(i):
                        copy.wait()

                @pl.when(i * PIECE >= length)
                def _():
                    latent[pl.ds(i * PIECE, PIECE), :] = jnp.zeros((PIECE, KVL), BF16)

            s = dot(latent[at, :], query_lat, 1, 1) + dot(rope[:, at], query_rope, 0, 1)
            position = c * CHUNK + lax.broadcasted_iota(jnp.int32, s.shape, 0)
            s = jnp.where(position < length, s, -1e30)
            scores[at, :] = s
            top[...] = jnp.maximum(top[...], jnp.max(s, axis=0, keepdims=True))

    for c in range(places // CHUNK):
        at = pl.ds(c * CHUNK, CHUNK)

        @pl.when(c * CHUNK < length)
        def _():
            p = jnp.exp2((scores[at, :] - top[...]) * scale)
            total[...] += jnp.sum(p, axis=0, keepdims=True)
            acc[...] += dot(p.astype(BF16), latent[at, :], 0, 0)

    sums = jnp.transpose(jnp.broadcast_to(total[...], (128, 128)))
    out_ref[...] = (acc[...] / sums[:, :1]).astype(BF16)


def value_kernel(latent_ref, value_up_ref, out_ref, wide_ref):
    heads = value_up_ref.shape[0]
    wide_ref[...] = latent_ref[...].astype(F32).reshape(wide_ref.shape)
    for h in range(heads):
        out_ref[:, h * VH : h * VH + VH] = dot(
            wide_ref[:, h, :].astype(BF16), value_up_ref[h]
        ).astype(BF16)


def output_kernel(holder_ref, own_ref, one_ref, two_ref, three_ref, pair_ref, proj_ref, out_ref):
    count = holder_ref.shape[1]
    gx = lax.axis_index("gx")
    core = lax.rem(gx, 2)
    z = lax.div(gx, 2)
    row = lax.broadcasted_iota(jnp.int32, (count, count), 1)
    slot = (
        (((row >> 4) & 3) ^ z) * 32
        + ((row >> 6) ^ core) * 16
        + (row & 15)
    )
    slots = lax.broadcasted_iota(jnp.int32, (count, count), 0)
    place = (slots == slot).astype(F32).astype(BF16)
    order = dot(holder_matrix(holder_ref[...]), place).astype(BF16)
    values = jnp.concatenate(
        [own_ref[...], one_ref[...], two_ref[...], three_ref[...], pair_ref[...]], axis=0
    )
    values = dot(order, values).astype(BF16)
    out_ref[...] = dot(values, proj_ref[...]).astype(BF16)


def call(kernel, out_shape, in_specs, scratch=(), limit=None, name=None):
    many = isinstance(out_shape, (list, tuple))
    return pl.pallas_call(
        kernel,
        out_shape=out_shape,
        in_specs=in_specs,
        out_specs=[VMEM] * len(out_shape) if many else VMEM,
        scratch_shapes=list(scratch),
        compiler_params=pltpu.CompilerParams(vmem_limit_bytes=limit) if limit else None,
        name=name,
    )


def swap(array, distance, axis="gx"):
    count = lax.axis_size(axis)
    return lax.ppermute(array, axis, [(i, i ^ distance) for i in range(count)])


def tables(lengths, holder, heads):
    half = ROPE // 2
    first = lax.axis_index("gx") * 16
    own = lax.dynamic_slice_in_dim(holder, first, 16, 0)
    own_lengths = jnp.sum(
        jnp.where(own[:, None] == jnp.arange(holder.shape[0])[None, :], lengths[None, :], 0), axis=1
    )
    frequency = 10000.0 ** (-2.0 * jnp.arange(half).astype(F32) / ROPE)
    angles = (own_lengths - 1).astype(F32)[:, None] * frequency
    cos, sin = jnp.cos(angles), jnp.sin(angles)
    ones = jnp.ones((16, NOPE), F32)
    none = jnp.zeros((16, NOPE), F32)
    blank = jnp.zeros((16, half), F32)
    keep = jnp.tile(jnp.concatenate([ones, cos, cos], axis=1), (1, heads))
    minus = jnp.tile(jnp.concatenate([none, -sin, blank], axis=1), (1, heads))
    plus = jnp.tile(jnp.concatenate([none, blank, sin], axis=1), (1, heads))
    return keep, minus, plus


def local(
    compressed, query_up, key_absorb, value_up, out_proj, cache_latent, cache_rope, lengths, holder
):
    shape = jax.ShapeDtypeStruct
    index_gx = lax.axis_index("gx")
    index_gy = lax.axis_index("gy")
    batch = compressed.shape[0]
    width = query_up.shape[1]
    heads = key_absorb.shape[0]
    places = cache_latent.shape[1]
    holder_row = holder.reshape(1, batch)
    slot = index_gx * 16 + index_gy
    length = jnp.sum(
        jnp.where(jnp.arange(batch) == lax.dynamic_slice_in_dim(holder, slot, 1, 0), lengths, 0)
    ).reshape(1)
    keep, minus, plus = tables(lengths, holder, heads)

    mine, other = call(
        project_kernel,
        (shape((64, width), F32), shape((64, width), BF16)),
        [VMEM] * 3,
        [pltpu.VMEM((batch, width), F32)],
        name="project",
    )(holder_row, compressed.T, query_up)
    got = swap(other, 1)
    own, one, two, three = call(
        pair_kernel,
        (shape((16, width), F32),) + (shape((16, width), BF16),) * 3,
        [VMEM] * 2,
        name="pair",
    )(mine, got)
    one, two, three = swap(one, 2), swap(two, 4), swap(three, 6)
    queries = call(
        absorb_kernel,
        shape((16 * heads, WIDE), BF16),
        [VMEM] * 8,
        [pltpu.VMEM((16, heads, WIDE), F32)],
        name="absorb",
    )(own, one, two, three, keep, minus, plus, key_absorb)
    queries = lax.all_to_all(queries, "gy", split_axis=0, concat_axis=0, tiled=True)

    latent_out = call(
        attend_kernel,
        shape((128, KVL), BF16),
        [SMEM, VMEM, ANY, ANY],
        [
            pltpu.VMEM((places, KVL), BF16),
            pltpu.VMEM((ROPE, places), BF16),
            pltpu.VMEM((places, 128), F32),
            pltpu.VMEM((1, 128), F32),
            pltpu.VMEM((1, 128), F32),
            pltpu.VMEM((128, KVL), F32),
            pltpu.SemaphoreType.DMA((2, places // PIECE)),
        ],
        limit=44 * 2**20,
        name="attend",
    )(length, queries, cache_latent, cache_rope)

    returned = lax.all_to_all(latent_out, "gy", split_axis=0, concat_axis=0, tiled=True)
    values = call(
        value_kernel,
        shape((16, heads * VH), BF16),
        [VMEM] * 2,
        [pltpu.VMEM((16, heads, KVL), F32)],
        name="values",
    )(returned, value_up)
    one, two, three = swap(values, 2), swap(values, 4), swap(values, 6)
    pair = swap(jnp.concatenate([values, one, two, three], axis=0), 1)
    partial = call(
        output_kernel,
        shape((batch, out_proj.shape[1]), BF16),
        [VMEM] * 7,
        name="output",
    )(holder_row, values, one, two, three, pair, out_proj)
    partial = lax.all_to_all(partial, "gy", split_axis=0, concat_axis=0, tiled=True)
    partial = partial.reshape(16, batch // 16, out_proj.shape[1])
    return jnp.sum(partial.astype(F32), axis=0).astype(BF16)


def solution(mesh):
    in_specs = (
        P(None, "gx"),
        P("gx", "gy"),
        P("gy", None, None),
        P("gy", None, None),
        P("gy", "gx"),
        P(("gx", "gy"), None, None),
        P(("gx", "gy"), None, None),
        P(),
        P(),
    )
    out_specs = P("gy", "gx")
    return jax.shard_map(local, mesh=mesh, in_specs=in_specs, out_specs=out_specs, check_vma=False)
```

time: 228 us -> 88.9 us (0.39)
  waiting for transfers between devices: 124 us -> 13.6 us
  matrix products: 37.2 us -> 0 us
  Pallas kernels: 0 us -> 22.5 us
  between operations: 16.1 us -> 0.17 us
  starting transfers between devices: 12.1 us -> 17.5 us
    unnamed x3 -> x0, waiting for transfers between devices: 78.8 us -> none
    dot_general x8 -> x0, matrix products: 37.2 us -> none  [the longest x1 14.5 us: attend(): lax.dot_general(query_lat, latent, (((1,), (1,)), ((), ())), preferred_el...]
    reduce_scatter x1 -> x0, waiting for transfers between devices: 29.6 us -> none  [local(): lax.psum_scatter(partial_sum, 'gx', scatter_dimension=1, tiled=True)]
    pallas_call x0 -> x6, Pallas kernels: none -> 22.5 us  [the longest x1 10.3 us: local(): call(attend_kernel, shape((128, KVL), BF16), [SMEM, VMEM, ANY, ANY], [plt...]
    all_gather x1 -> x0, blocking collectives: 12.8 us -> none  [local(): all_values = lax.all_gather(head_values, 'gx', axis=1, tiled=True)]
    all_to_all x1 -> x2, blocking collectives: 14.2 us -> 25.2 us  [the longest x1 12.9 us: local(): lax.all_to_all(latent_out, 'gy', split_axis=0, concat_axis=0, tiled=True)]
    ppermute x0 -> x8, starting transfers between devices: none -> 10.4 us  [swap(): return lax.ppermute(array, axis, [(i, i ^ distance) for i in range(count)])]
    all_to_all x2 -> x1, waiting for transfers between devices: 15.2 us -> 6.06 us  [local(): lax.all_to_all(queries, 'gy', split_axis=0, concat_axis=0, tiled=True)]
  transfers between devices with their start and end apart: 4 -> 9, of which waited for: 4 -> 6; matrix products, arithmetic and copies ran while one was open for 3% -> 7% of each run, Pallas kernels for 0% -> 0%
where the time goes in v1:
time: 88.9 us; the launch traced here: 88.3 us
  blocking collectives  25.2 us (28%)
  Pallas kernels  22.5 us (25%)
  starting transfers between devices  17.5 us (20%)
  waiting for transfers between devices  13.6 us (15%)
  local copies, waits for them, and re-layouts  5.65 us (6%)
  other arithmetic  3.74 us (4%)
    all_to_all x1, blocking collectives, local(): lax.all_to_all(latent_out, 'gy', split_axis=0, concat_axis=0, tiled=True)  12.9 us
    all_to_all x1, blocking collectives, local(): lax.all_to_all(partial, 'gy', split_axis=0, concat_axis=0, tiled=True)  12.2 us
    ppermute x8, starting transfers between devices, swap(): return lax.ppermute(array, axis, [(i, i ^ distance) for i in range(count)])  10.4 us
    pallas_call x1, Pallas kernels, local(): call(attend_kernel, shape((128, KVL), BF16), [SMEM, VMEM, ANY, ANY], [plt...  10.3 us
    ppermute x8, waiting for transfers between devices, swap(): return lax.ppermute(array, axis, [(i, i ^ distance) for i in range(count)])  7.52 us
    all_to_all x1, starting transfers between devices, local(): lax.all_to_all(queries, 'gy', split_axis=0, concat_axis=0, tiled=True)  7.03 us
    all_to_all x1, waiting for transfers between devices, local(): lax.all_to_all(queries, 'gy', split_axis=0, concat_axis=0, tiled=True)  6.06 us
    pallas_call x1, Pallas kernels, local(): call(output_kernel, shape((batch, out_proj.shape[1]), BF16), [VMEM] * 7,...  3.07 us
  transfers between devices with their start and end apart: 9, of which 6 were waited for; matrix products, arithmetic and copies ran while one was open for 7% of the time, Pallas kernels for 0%

profile of v1, /device:TPU:0, one launch (start us, length us, event | category | flops | bytes accessed | tf_op | source)
XLA Modules:
  0.0 88.3 jit_solution(1008671175969611961)
XLA Ops:
  0.0 2.4 %project.1 = (f32[64,1536]{1,0:T(8,128)}, bf16[64,1536]{1,0:T(8,128)(2,1)}) custom-call(s32[1,128]{1,0:T(1,128)} %bitcast.15, bf16[192,128]{1,0:T(8,128)(2,1)} %bitcast.14, bf16[192,1536]{1,0:T(8,128)(2,1)} %query_up_ref.1), custom_call_target="tpu_custom_call" | custom-call | tf_op jit(solution)/shard_map/project/pallas_call | solution.py:233
  2.6 0.9 dynamic_slice.7
  3.4 0.8 select_reduce_fusion
  4.3 0.1 multiply_sine_fusion
  4.5 0.7 copy-done.1
  5.1 1.8 %pair.1 = (f32[16,1536]{1,0:T(8,128)}, bf16[16,1536]{1,0:T(8,128)(2,1)}, bf16[16,1536]{1,0:T(8,128)(2,1)}, bf16[16,1536]{1,0:T(8,128)(2,1)}) custom-call(f32[64,1536]{1,0:T(8,128)} %get-tuple-element.11.mine_ref, bf16[64,1536]{1,0:T(8,128)(2,1)} %copy-done.1), custom_call_target="tpu_custom_call" | custom-call | tf_op jit(solution)/shard_map/pair/pallas_call | solution.py:241
  6.9 2.0 %collective-permute-start.1 = (bf16[16,1536]{1,0:T(8,128)(2,1)}, bf16[16,1536]{1,0:T(8,128)(2,1)S(1)}, u32[]{:S(2)}, u32[]{:S(2)}) collective-permute-start(bf16[16,1536]{1,0:T(8,128)(2,1)} %get-tuple-element.14), channel_id=1, source_target_pairs={{0,32},{16,48},{32,0},{48,16},{64,96},{80,112},{96,64},{112,80},{1... | collective-permute-start | bytes 147464 | tf_op jit(solution)/shard_map/ppermute | solution.py:194
  8.9 3.6 %collective-permute-start.2 = (bf16[16,1536]{1,0:T(8,128)(2,1)}, bf16[16,1536]{1,0:T(8,128)(2,1)S(1)}, u32[]{:S(2)}, u32[]{:S(2)}) collective-permute-start(bf16[16,1536]{1,0:T(8,128)(2,1)} %get-tuple-element.15), channel_id=1, source_target_pairs={{0,64},{16,80},{32,96},{48,112},{64,0},{80,16},{96,32},{112,48},{1... | collective-permute-start | bytes 147464 | tf_op jit(solution)/shard_map/ppermute | solution.py:194
  12.6 0.7 tile.13.keep_ref
  13.3 0.7 tile.30.minus_ref
  14.1 0.7 tile.32.plus_ref
  14.8 0.9 %collective-permute-done.2.two_ref = bf16[16,1536]{1,0:T(8,128)(2,1)S(1)} collective-permute-done((bf16[16,1536]{1,0:T(8,128)(2,1)}, bf16[16,1536]{1,0:T(8,128)(2,1)S(1)}, u32[]{:S(2)}, u32[]{:S(2)}) %collective-permute-start.2) | collective-permute-done | bytes 49184 | tf_op jit(solution)/shard_map/ppermute | solution.py:194
  15.7 2.3 %collective-permute-done.3.three_ref = bf16[16,1536]{1,0:T(8,128)(2,1)S(1)} collective-permute-done((bf16[16,1536]{1,0:T(8,128)(2,1)}, bf16[16,1536]{1,0:T(8,128)(2,1)S(1)}, u32[]{:S(2)}, u32[]{:S(2)}) %collective-permute-start.3) | collective-permute-done | bytes 49184 | tf_op jit(solution)/shard_map/ppermute | solution.py:194
  18.0 0.6 copy-done.8
  18.6 2.6 %absorb.1 = bf16[128,640]{1,0:T(8,128)(2,1)} custom-call(f32[16,1536]{1,0:T(8,128)} %get-tuple-element.13.own_ref, bf16[16,1536]{1,0:T(8,128)(2,1)} %copy-done.6, bf16[16,1536]{1,0:T(8,128)(2,1)} %copy-done.7, bf16[16,1536]{1,0:T(8,128)(2,1)} %copy-done.8, f32[16,1536]{1,0:T(8,128)} %tile.13.keep_ref, f32[16,1536]{1,0:T(8,128)} %tile.30.minus_ref, ...), custom_call_target="tpu_custom_call" | custom-call | tf_op jit(solution)/shard_map/absorb/pallas_call | solution.py:248
  21.2 7.0 %all-to-all-start = ((bf16[16,8,640]{2,1,0:T(8,128)(2,1)}), bf16[16,8,640]{2,1,0:T(8,128)(2,1)S(1)}, u32[]{:S(2)}, u32[]{:S(2)}) async-start(bf16[16,8,640]{2,1,0:T(8,128)(2,1)} %bitcast.12), calls=%async_computation | async-start | bytes 327680 | tf_op jit(solution)/shard_map/all_to_all | solution.py:255
  28.3 0.6 dynamic_slice.6
  28.9 1.3 %fusion.1 = s32[]{:T(128)} fusion(s32[128]{0:T(128)S(1)} %copy-done.10, s32[]{:T(128)} %bitcast.1), kind=kLoop, calls=%fused_computation.10 | loop fusion | flops 383 | bytes 520 | tf_op jit(solution)/shard_map/reduce_sum | solution.py:228
  30.1 6.1 %all-to-all-done = bf16[16,8,640]{2,1,0:T(8,128)(2,1)S(1)} async-done(((bf16[16,8,640]{2,1,0:T(8,128)(2,1)}), bf16[16,8,640]{2,1,0:T(8,128)(2,1)S(1)}, u32[]{:S(2)}, u32[]{:S(2)}) %all-to-all-start) | async-done | bytes 163872 | tf_op jit(solution)/shard_map/all_to_all | solution.py:255
  36.2 10.3 %attend.1 = bf16[128,512]{1,0:T(8,128)(2,1)S(1)} custom-call(s32[1]{0:T(128)} %bitcast.2.length_ref, bf16[128,640]{1,0:T(8,128)(2,1)S(1)} %bitcast.9, bf16[1,16384,512]{2,1,0:T(8,128)(2,1)} %latent_hbm.1, bf16[1,64,16384]{2,1,0:T(8,128)(2,1)S(1)} %copy-done), custom_call_target="tpu_custom_call" | custom-call | tf_op jit(solution)/shard_map/attend/pallas_call | solution.py:257
  46.6 12.9 %all_to_all.31 = bf16[16,8,512]{2,1,0:T(8,128)(2,1)} all-to-all(bf16[16,8,512]{2,1,0:T(8,128)(2,1)S(1)} %bitcast.10), channel_id=1, replica_groups=mesh['gx'=8,'gy'=16] {'gy'}, dimensions={0} | all-to-all | bytes 262144 | tf_op jit(solution)/shard_map/all_to_all | solution.py:274
  59.5 2.3 %values.1.own_ref = bf16[16,1024]{1,0:T(8,128)(2,1)} custom-call(bf16[128,512]{1,0:T(8,128)(2,1)} %bitcast.13, bf16[8,512,128]{2,1,0:T(8,128)(2,1)} %value_up_ref.1), custom_call_target="tpu_custom_call" | custom-call | tf_op jit(solution)/shard_map/values/pallas_call | solution.py:275
  61.8 2.3 %collective-permute-start.5 = (bf16[16,1024]{1,0:T(8,128)(2,1)}, bf16[16,1024]{1,0:T(8,128)(2,1)S(1)}, u32[]{:S(2)}, u32[]{:S(2)}) collective-permute-start(bf16[16,1024]{1,0:T(8,128)(2,1)} %values.1.own_ref), channel_id=1, source_target_pairs={{0,64},{16,80},{32,96},{48,112},{64,0},{80,16},{96,32},{112,48},{1... | collective-permute-start | bytes 98312 | tf_op jit(solution)/shard_map/ppermute | solution.py:194
  64.2 2.3 %collective-permute-start.6 = (bf16[16,1024]{1,0:T(8,128)(2,1)}, bf16[16,1024]{1,0:T(8,128)(2,1)S(1)}, u32[]{:S(2)}, u32[]{:S(2)}) collective-permute-start(bf16[16,1024]{1,0:T(8,128)(2,1)} %values.1.own_ref), channel_id=1, source_target_pairs={{0,96},{16,112},{32,64},{48,80},{64,32},{80,48},{96,0},{112,16},{1... | collective-permute-start | bytes 98312 | tf_op jit(solution)/shard_map/ppermute | solution.py:194
  66.5 0.9 %collective-permute-done.5.two_ref = bf16[16,1024]{1,0:T(8,128)(2,1)S(1)} collective-permute-done((bf16[16,1024]{1,0:T(8,128)(2,1)}, bf16[16,1024]{1,0:T(8,128)(2,1)S(1)}, u32[]{:S(2)}, u32[]{:S(2)}) %collective-permute-start.5) | collective-permute-done | bytes 32800 | tf_op jit(solution)/shard_map/ppermute | solution.py:194
  67.5 2.1 %collective-permute-done.6.three_ref = bf16[16,1024]{1,0:T(8,128)(2,1)S(1)} collective-permute-done((bf16[16,1024]{1,0:T(8,128)(2,1)}, bf16[16,1024]{1,0:T(8,128)(2,1)S(1)}, u32[]{:S(2)}, u32[]{:S(2)}) %collective-permute-start.6) | collective-permute-done | bytes 32800 | tf_op jit(solution)/shard_map/ppermute | solution.py:194
  69.5 0.8 pad_maximum_fusion
  70.4 1.3 %collective-permute-done.7.pair_ref = bf16[64,1024]{1,0:T(8,128)(2,1)S(1)} collective-permute-done((bf16[64,1024]{1,0:T(8,128)(2,1)S(1)}, bf16[64,1024]{1,0:T(8,128)(2,1)S(1)}, u32[]{:S(2)}, u32[]{:S(2)}) %collective-permute-start.7) | collective-permute-done | bytes 131104 | tf_op jit(solution)/shard_map/ppermute | solution.py:194
  71.7 0.6 copy-done.5
  72.4 3.1 %output.1 = bf16[128,896]{1,0:T(8,128)(2,1)} custom-call(s32[1,128]{1,0:T(1,128)} %bitcast.16, bf16[16,1024]{1,0:T(8,128)(2,1)} %values.1.own_ref, bf16[16,1024]{1,0:T(8,128)(2,1)} %copy-done.2, bf16[16,1024]{1,0:T(8,128)(2,1)} %copy-done.3, bf16[16,1024]{1,0:T(8,128)(2,1)} %copy-done.4, bf16[64,1024]{1,0:T(8,128)(2,1)} %copy-done.5, bf16[1024,896]{1,0:T(8,128)(2,1)} %proj_ref.1), custom_call_target="tpu_custom_call" | custom-call | tf_op jit(solution)/shard_map/output/pallas_call | solution.py:284
  75.5 12.2 %all_to_all.32 = bf16[16,8,896]{2,1,0:T(8,128)(2,1)S(1)} all-to-all(bf16[16,8,896]{2,1,0:T(8,128)(2,1)} %bitcast.11), channel_id=1, replica_groups=mesh['gx'=8,'gy'=16] {'gy'}, dimensions={0} | all-to-all | bytes 458752 | tf_op jit(solution)/shard_map/all_to_all | solution.py:290
  87.7 0.6 reduce_sum.32
  (37 shorter events, 0.3 us)
Async XLA Ops:
  2.4 25.8 %copy-start.9 = (s32[128]{0:T(128)S(1)}, s32[128]{0:T(128)}, u32[]{:S(2)}) copy-start(s32[128]{0:T(128)} %param.17) | copy-start | bytes 1540
  2.4 26.4 %copy-start.10 = (s32[128]{0:T(128)S(1)}, s32[128]{0:T(128)}, u32[]{:S(2)}) copy-start(s32[128]{0:T(128)} %param.16) | copy-start | bytes 1540
  2.4 33.8 %copy-start = (bf16[1,64,16384]{2,1,0:T(8,128)(2,1)S(1)}, bf16[1,64,16384]{2,1,0:T(8,128)(2,1)}, u32[]{:S(2)}) copy-start(bf16[1,64,16384]{2,1,0:T(8,128)(2,1)} %rope_hbm.1) | copy-start | bytes 6291460
  2.5 2.0 %collective-permute-start = (bf16[64,1536]{1,0:T(8,128)(2,1)}, bf16[64,1536]{1,0:T(8,128)(2,1)S(1)}, u32[]{:S(2)}, u32[]{:S(2)}) collective-permute-start(bf16[64,1536]{1,0:T(8,128)(2,1)} %get-tuple-element.12), channel_id=1, source_target_pairs={{0,16},{16,0},{32,48},{48,32},{64,80},{80,64},{96,112},{112,96},{1... | collective-permute-start | bytes 589832 | tf_op jit(solution)/shard_map/ppermute | solution.py:194
  4.4 0.7 copy-start.1
  6.9 7.9 %collective-permute-start.1 = (bf16[16,1536]{1,0:T(8,128)(2,1)}, bf16[16,1536]{1,0:T(8,128)(2,1)S(1)}, u32[]{:S(2)}, u32[]{:S(2)}) collective-permute-start(bf16[16,1536]{1,0:T(8,128)(2,1)} %get-tuple-element.14), channel_id=1, source_target_pairs={{0,32},{16,48},{32,0},{48,16},{64,96},{80,112},{96,64},{112,80},{1... | collective-permute-start | bytes 147464 | tf_op jit(solution)/shard_map/ppermute | solution.py:194
  8.9 6.8 %collective-permute-start.2 = (bf16[16,1536]{1,0:T(8,128)(2,1)}, bf16[16,1536]{1,0:T(8,128)(2,1)S(1)}, u32[]{:S(2)}, u32[]{:S(2)}) collective-permute-start(bf16[16,1536]{1,0:T(8,128)(2,1)} %get-tuple-element.15), channel_id=1, source_target_pairs={{0,64},{16,80},{32,96},{48,112},{64,0},{80,16},{96,32},{112,48},{1... | collective-permute-start | bytes 147464 | tf_op jit(solution)/shard_map/ppermute | solution.py:194
  12.5 5.5 %collective-permute-start.3 = (bf16[16,1536]{1,0:T(8,128)(2,1)}, bf16[16,1536]{1,0:T(8,128)(2,1)S(1)}, u32[]{:S(2)}, u32[]{:S(2)}) collective-permute-start(bf16[16,1536]{1,0:T(8,128)(2,1)} %get-tuple-element.16), channel_id=1, source_target_pairs={{0,96},{16,112},{32,64},{48,80},{64,32},{80,48},{96,0},{112,16},{1... | collective-permute-start | bytes 147464 | tf_op jit(solution)/shard_map/ppermute | solution.py:194
  14.8 3.2 %copy-start.6 = (bf16[16,1536]{1,0:T(8,128)(2,1)}, bf16[16,1536]{1,0:T(8,128)(2,1)S(1)}, u32[]{:S(2)}) copy-start(bf16[16,1536]{1,0:T(8,128)(2,1)S(1)} %collective-permute-done.1.one_ref) | copy-start | bytes 147460
  15.7 2.3 %copy-start.7 = (bf16[16,1536]{1,0:T(8,128)(2,1)}, bf16[16,1536]{1,0:T(8,128)(2,1)S(1)}, u32[]{:S(2)}) copy-start(bf16[16,1536]{1,0:T(8,128)(2,1)S(1)} %collective-permute-done.2.two_ref) | copy-start | bytes 147460
  18.0 0.6 copy-start.8
  21.2 15.0 %all-to-all-start = ((bf16[16,8,640]{2,1,0:T(8,128)(2,1)}), bf16[16,8,640]{2,1,0:T(8,128)(2,1)S(1)}, u32[]{:S(2)}, u32[]{:S(2)}) async-start(bf16[16,8,640]{2,1,0:T(8,128)(2,1)} %bitcast.12), calls=%async_computation | async-start | bytes 327680 | tf_op jit(solution)/shard_map/all_to_all | solution.py:255
  61.8 4.7 %collective-permute-start.4 = (bf16[16,1024]{1,0:T(8,128)(2,1)}, bf16[16,1024]{1,0:T(8,128)(2,1)S(1)}, u32[]{:S(2)}, u32[]{:S(2)}) collective-permute-start(bf16[16,1024]{1,0:T(8,128)(2,1)} %values.1.own_ref), channel_id=1, source_target_pairs={{0,32},{16,48},{32,0},{48,16},{64,96},{80,112},{96,64},{112,80},{1... | collective-permute-start | bytes 98312 | tf_op jit(solution)/shard_map/ppermute | solution.py:194
  61.8 5.6 %collective-permute-start.5 = (bf16[16,1024]{1,0:T(8,128)(2,1)}, bf16[16,1024]{1,0:T(8,128)(2,1)S(1)}, u32[]{:S(2)}, u32[]{:S(2)}) collective-permute-start(bf16[16,1024]{1,0:T(8,128)(2,1)} %values.1.own_ref), channel_id=1, source_target_pairs={{0,64},{16,80},{32,96},{48,112},{64,0},{80,16},{96,32},{112,48},{1... | collective-permute-start | bytes 98312 | tf_op jit(solution)/shard_map/ppermute | solution.py:194
  64.2 5.3 %collective-permute-start.6 = (bf16[16,1024]{1,0:T(8,128)(2,1)}, bf16[16,1024]{1,0:T(8,128)(2,1)S(1)}, u32[]{:S(2)}, u32[]{:S(2)}) collective-permute-start(bf16[16,1024]{1,0:T(8,128)(2,1)} %values.1.own_ref), channel_id=1, source_target_pairs={{0,96},{16,112},{32,64},{48,80},{64,32},{80,48},{96,0},{112,16},{1... | collective-permute-start | bytes 98312 | tf_op jit(solution)/shard_map/ppermute | solution.py:194
  66.5 5.2 %copy-start.2 = (bf16[16,1024]{1,0:T(8,128)(2,1)}, bf16[16,1024]{1,0:T(8,128)(2,1)S(1)}, u32[]{:S(2)}) copy-start(bf16[16,1024]{1,0:T(8,128)(2,1)S(1)} %collective-permute-done.4.one_ref) | copy-start | bytes 98308
  67.5 4.3 %copy-start.3 = (bf16[16,1024]{1,0:T(8,128)(2,1)}, bf16[16,1024]{1,0:T(8,128)(2,1)S(1)}, u32[]{:S(2)}) copy-start(bf16[16,1024]{1,0:T(8,128)(2,1)S(1)} %collective-permute-done.5.two_ref) | copy-start | bytes 98308
  69.5 2.2 %copy-start.4 = (bf16[16,1024]{1,0:T(8,128)(2,1)}, bf16[16,1024]{1,0:T(8,128)(2,1)S(1)}, u32[]{:S(2)}) copy-start(bf16[16,1024]{1,0:T(8,128)(2,1)S(1)} %collective-permute-done.6.three_ref) | copy-start | bytes 98308
  70.3 1.4 %collective-permute-start.7 = (bf16[64,1024]{1,0:T(8,128)(2,1)S(1)}, bf16[64,1024]{1,0:T(8,128)(2,1)S(1)}, u32[]{:S(2)}, u32[]{:S(2)}) collective-permute-start(bf16[64,1024]{1,0:T(8,128)(2,1)S(1)} %pad_maximum_fusion), channel_id=1, source_target_pairs={{0,16},{16,0},{32,48},{48,32},{64,80},{80,64},{96,112},{112,96},{1... | collective-permute-start | bytes 393224 | tf_op jit(solution)/shard_map/ppermute | solution.py:194
  71.7 0.7 copy-start.5

commit v2 on v0

v2 whole, which is shorter than its diff:
```python
import math

import jax
import jax.numpy as jnp
import numpy as np
from jax import lax
from jax.experimental import pallas as pl
from jax.experimental.pallas import tpu as pltpu
from jax.sharding import Mesh
from jax.sharding import PartitionSpec as P

KVL = 512
ROPE = 64
NOPE = 128
HEAD = NOPE + ROPE
VH = 128
WIDE = 640
CHUNK = 4096
PARTS = 4
VMEM = pl.BlockSpec(memory_space=pltpu.VMEM)
SMEM = pl.BlockSpec(memory_space=pltpu.SMEM)
ANY = pl.BlockSpec(memory_space=pl.ANY)
F32 = jnp.float32
BF16 = jnp.bfloat16


def dot(a, b, contract_a=1, contract_b=0):
    return lax.dot_general(
        a, b, (((contract_a,), (contract_b,)), ((), ())), preferred_element_type=F32
    )


def holder_matrix(holder_row):
    count = holder_row.shape[1]
    requests = lax.broadcasted_iota(jnp.int32, (count, count), 0)
    return (requests == holder_row).astype(F32).astype(BF16)


def order_matrix(holder_row):
    count = holder_row.shape[1]
    row = lax.broadcasted_iota(jnp.int32, (count, count), 1)
    core = (row >> 6) ^ lax.axis_index("c")
    slot = ((row & 3) * 2 + core) * 16 + ((row >> 2) & 15)
    slots = lax.broadcasted_iota(jnp.int32, (count, count), 0)
    place = (slots == slot).astype(F32).astype(BF16)
    return dot(holder_matrix(holder_row), place).astype(BF16)


def project_kernel(
    holder_hbm, compressed_hbm, query_up_hbm, mine_ref, other_ref, holder, compressed, query_up, sems
):
    half, width = mine_ref.shape
    part = width // PARTS
    copies = [
        pltpu.make_async_copy(holder_hbm, holder, sems.at[0]),
        pltpu.make_async_copy(compressed_hbm, compressed, sems.at[1]),
    ]
    for i in range(PARTS):
        at = pl.ds(i * part, part)
        copies.append(
            pltpu.make_async_copy(query_up_hbm.at[:, at], query_up.at[:, at], sems.at[2 + i])
        )
    for copy in copies:
        copy.start()
    copies[0].wait()
    order = order_matrix(holder[...])
    copies[1].wait()
    by_slot = dot(compressed[...], order).astype(BF16)
    for i in range(PARTS):
        at = slice(i * part, i * part + part)
        copies[2 + i].wait()
        term = dot(by_slot, query_up[:, at], 0, 0)
        mine_ref[:, at] = term[:half]
        other_ref[:, at] = term[half:].astype(BF16)


def prepare_kernel(
    holder_ref, lengths_ref, frequency_ref, absorb_hbm, angle_ref, absorb_ref, place_ref, sem
):
    copy = pltpu.make_async_copy(absorb_hbm, absorb_ref, sem)
    copy.start()
    core = lax.axis_index("c")
    for j in range(place_ref.shape[0]):
        slot = ((j & 3) * 2 + core) * 16 + (j >> 2)
        place = (lengths_ref[holder_ref[slot]] - 1).astype(F32)
        place_ref[j : j + 1, :] = jnp.full((1, 128), place, F32)
    angles = place_ref[...] * frequency_ref[...]
    sin = jnp.sin(angles)
    lane = lax.broadcasted_iota(jnp.int32, angles.shape, 1)
    former = (lane & (ROPE - 1)) < ROPE // 2
    angle_ref[0] = jnp.cos(angles)
    angle_ref[1] = jnp.where(former, -sin, 0.0)
    angle_ref[2] = jnp.where(former, 0.0, sin)
    copy.wait()


def absorb_kernel(
    mine_ref, got_ref, angle_ref, absorb_ref, latent_hbm, rope_hbm, out_ref, wide_ref
):
    queries = mine_ref[...] + got_ref[...].astype(F32)
    lane = lax.broadcasted_iota(jnp.int32, (queries.shape[0], 128), 1)
    low = lane < 64
    for h in range(0, absorb_ref.shape[0], 2):
        start = h * HEAD
        first = queries[:, start : start + 128]
        second = queries[:, start + 128 : start + 256]
        third = queries[:, start + 256 : start + 384]
        other = pltpu.roll(jnp.where(low, third, second), 64, 1)
        rope = jnp.where(low, second, third)
        rope = (
            rope * angle_ref[0]
            + pltpu.roll(rope, 128 - ROPE // 2, 1) * angle_ref[1]
            + pltpu.roll(rope, ROPE // 2, 1) * angle_ref[2]
        )
        wide_ref[:, h, :KVL] = dot(first.astype(BF16), absorb_ref[h])
        wide_ref[:, h, KVL:] = jnp.where(low, rope, 0.0)
        wide_ref[:, h + 1, :KVL] = dot(other.astype(BF16), absorb_ref[h + 1])
        wide_ref[:, h + 1, KVL:] = jnp.where(low, 0.0, rope)
    out_ref[...] = wide_ref[...].reshape(out_ref.shape).astype(BF16)


def attend_kernel(holder_ref, lengths_ref, query_ref, latent, rope, out_ref, scores):
    slot = (lax.axis_index("z") * 2 + lax.axis_index("c")) * 16
    slot += lax.axis_index("x") * 4 + lax.axis_index("y")
    length = lengths_ref[holder_ref[slot]]
    places = latent.shape[1]
    groups, chips, heads = out_ref.shape[:3]
    count = groups * heads

    query = query_ref[:, 0].astype(F32)
    for z in range(1, chips):
        query += query_ref[:, z].astype(F32)
    query = query.reshape(count, WIDE) * (math.log2(math.e) / math.sqrt(HEAD))
    query_lat = query[:, :KVL].astype(BF16)
    query_rope = (query[:, KVL : KVL + ROPE] + query[:, KVL + ROPE :]).astype(BF16)
    tops = []
    for start in range(0, places, CHUNK):
        at = slice(start, start + CHUNK)
        s = dot(latent[0, at, :], query_lat, 1, 1) + dot(rope[0, :, at], query_rope, 0, 1)
        position = start + lax.broadcasted_iota(jnp.int32, s.shape, 0)
        s = jnp.where(position < length, s, -1e30)
        scores[at, :] = s
        tops.append(jnp.max(s, axis=0, keepdims=True))
    top = tops[0]
    for other in tops[1:]:
        top = jnp.maximum(top, other)
    total = jnp.zeros((1, count), F32)
    acc = jnp.zeros((count, KVL), F32)
    for start in range(0, places, CHUNK):
        at = slice(start, start + CHUNK)
        p = jnp.exp2(scores[at, :] - top)
        total += jnp.sum(p, axis=0, keepdims=True)
        acc += dot(p.astype(BF16), latent[0, at, :], 0, 0)
    total = jnp.transpose(jnp.broadcast_to(total, (count, count)))[:, :1]
    result = (acc / total).reshape(groups, heads, KVL).astype(BF16)
    for z in range(chips):
        out_ref[:, z] = result


def value_kernel(latent_ref, value_up_ref, out_ref, wide_ref):
    heads = value_up_ref.shape[0]
    wide_ref[...] = latent_ref[...].astype(F32).reshape(wide_ref.shape)
    for h in range(heads):
        out_ref[:, h * VH : h * VH + VH] = dot(
            wide_ref[:, h, :].astype(BF16), value_up_ref[h]
        ).astype(BF16)


def output_kernel(holder_ref, own_ref, pair_ref, proj_ref, out_ref):
    values = jnp.concatenate([own_ref[...], pair_ref[...]], axis=0)
    values = dot(order_matrix(holder_ref[...]), values).astype(BF16)
    out_ref[...] = dot(values, proj_ref[...]).astype(BF16)


def call(kernel, out_shape, in_specs, scratch=(), limit=8, name=None, cost=None):
    many = isinstance(out_shape, (list, tuple))
    return pl.pallas_call(
        kernel,
        out_shape=out_shape,
        in_specs=in_specs,
        out_specs=[VMEM] * len(out_shape) if many else VMEM,
        scratch_shapes=list(scratch),
        compiler_params=pltpu.CompilerParams(vmem_limit_bytes=limit * 2**20),
        name=name,
        cost_estimate=cost,
    )


def stay(array):
    return pltpu.with_memory_space_constraint(array, pltpu.HBM)


def keep(array):
    return pltpu.with_memory_space_constraint(array, pltpu.VMEM)


def swap_cores(array):
    return lax.ppermute(array, "c", [(0, 1), (1, 0)])


def exchange(array, axes):
    return lax.all_to_all(array, axes, split_axis=0, concat_axis=0, tiled=True)


def local(
    compressed, query_up, key_absorb, value_up, out_proj, cache_latent, cache_rope, lengths, holder
):
    shape = jax.ShapeDtypeStruct
    batch = compressed.shape[0]
    width = query_up.shape[1]
    heads = key_absorb.shape[0]
    places = cache_latent.shape[1]
    chips = lax.axis_size("z")
    groups = lax.axis_size("x") * lax.axis_size("y")
    own = chips * groups
    holder_row = holder.reshape(1, batch)
    half = np.arange(ROPE // 2, dtype=np.float32)
    frequency = (10000.0 ** (-2.0 * half / ROPE)).astype(np.float32)
    frequency = jnp.asarray(np.tile(frequency, 4)[None, :])

    mine, other = call(
        project_kernel,
        (pltpu.VMEM((own, width), F32), pltpu.VMEM((own, width), BF16)),
        [ANY] * 3,
        [
            pltpu.VMEM((1, batch), jnp.int32),
            pltpu.VMEM((compressed.shape[1], batch), BF16),
            pltpu.VMEM(query_up.shape, BF16),
            pltpu.SemaphoreType.DMA((2 + PARTS,)),
        ],
        name="project",
    )(stay(holder_row), stay(compressed.T), stay(query_up))
    got = swap_cores(other)
    angles, absorb_in = call(
        prepare_kernel,
        (pltpu.VMEM((3, own, 128), F32), pltpu.VMEM(key_absorb.shape, BF16)),
        [SMEM, SMEM, VMEM, ANY],
        [pltpu.VMEM((own, 128), F32), pltpu.SemaphoreType.DMA],
        name="prepare",
    )(stay(holder), stay(lengths), stay(frequency), stay(key_absorb))
    queries = call(
        absorb_kernel,
        shape((own * heads, WIDE), BF16),
        [VMEM] * 4 + [ANY] * 2,
        [pltpu.VMEM((own, heads, WIDE), F32)],
        name="absorb",
    )(mine, got, angles, absorb_in, stay(cache_latent), stay(cache_rope))
    queries = exchange(queries, ("x", "y", "z"))

    latent_out = call(
        attend_kernel,
        shape((groups, chips, heads, KVL), BF16),
        [SMEM, SMEM, VMEM, VMEM, VMEM],
        [pltpu.VMEM((places, 128), F32)],
        limit=20,
        name="attend",
    )(
        holder,
        lengths,
        queries.reshape(groups, chips, heads, WIDE),
        keep(cache_latent),
        keep(cache_rope),
    )

    returned = exchange(latent_out.reshape(own * heads, KVL), ("x", "y", "z"))
    values = call(
        value_kernel,
        shape((own, heads * VH), BF16),
        [VMEM] * 2,
        [pltpu.VMEM((own, heads, KVL), F32)],
        name="values",
    )(returned, value_up)
    partial = call(
        output_kernel,
        shape((batch, out_proj.shape[1]), BF16),
        [VMEM] * 4,
        name="output",
    )(holder_row, values, swap_cores(values), out_proj)
    partial = exchange(partial, ("x", "y"))
    partial = partial.reshape(groups, batch // groups, out_proj.shape[1])
    return jnp.sum(partial.astype(F32), axis=0).astype(BF16)


def solution(mesh):
    mesh = Mesh(mesh.devices.reshape(4, 2, 4, 4), ("z", "c", "x", "y"))
    gx, gy, both = ("z", "c"), ("x", "y"), ("z", "c", "x", "y")
    in_specs = (
        P(None, gx),
        P(gx, gy),
        P(gy, None, None),
        P(gy, None, None),
        P(gy, gx),
        P(both, None, None),
        P(both, None, None),
        P(),
        P(),
    )
    out_specs = P(gy, gx)
    return jax.shard_map(local, mesh=mesh, in_specs=in_specs, out_specs=out_specs, check_vma=False)
```

time: 228 us -> 74.5 us (0.33)
  waiting for transfers between devices: 124 us -> 1.34 us
  matrix products: 37.2 us -> 0 us
  blocking collectives: 27.1 us -> 55.3 us
  Pallas kernels: 0 us -> 16.7 us
  between operations: 16.1 us -> 0.12 us
  starting transfers between devices: 12.1 us -> 0.15 us
  local copies, waits for them, and re-layouts: 6.67 us -> 0.04 us
  other arithmetic: 5.03 us -> 0.64 us
    unnamed x3 -> x0, waiting for transfers between devices: 78.8 us -> none
    all_to_all x1 -> x3, blocking collectives: 14.2 us -> 55.3 us  [exchange(): return lax.all_to_all(array, axes, split_axis=0, concat_axis=0, tiled=True)]
    dot_general x8 -> x0, matrix products: 37.2 us -> none  [the longest x1 14.5 us: attend(): lax.dot_general(query_lat, latent, (((1,), (1,)), ((), ())), preferred_el...]
    reduce_scatter x1 -> x0, waiting for transfers between devices: 29.6 us -> none  [local(): lax.psum_scatter(partial_sum, 'gx', scatter_dimension=1, tiled=True)]
    pallas_call x0 -> x6, Pallas kernels: none -> 16.7 us  [the longest x1 10.3 us: local(): call(attend_kernel, shape((groups, chips, heads, KVL), BF16), [SMEM, SMEM...]
    all_to_all x2 -> x0, waiting for transfers between devices: 15.2 us -> none  [the longest x1 8.88 us: local(): lax.all_to_all(send_lat, ('gx', 'gy'), split_axis=0, concat_axis=1, tiled...]
    all_gather x1 -> x0, blocking collectives: 12.8 us -> none  [local(): all_values = lax.all_gather(head_values, 'gx', axis=1, tiled=True)]
    all_to_all x2 -> x0, starting transfers between devices: 12 us -> none  [the longest x1 7.42 us: local(): lax.all_to_all(send_rope, ('gx', 'gy'), split_axis=0, concat_axis=1, tile...]
  transfers between devices with their start and end apart: 4 -> 2, of which waited for: 4 -> 1; matrix products, arithmetic and copies ran while one was open for 3% -> 0% of each run, Pallas kernels for 0% -> 3%
where the time goes in v2:
time: 74.5 us; the launch traced here: 74.2 us
  blocking collectives  55.3 us (74%)
  Pallas kernels  16.7 us (22%)
  waiting for transfers between devices  1.34 us (2%)
    all_to_all x3, blocking collectives, exchange(): return lax.all_to_all(array, axes, split_axis=0, concat_axis=0, tiled=True)  55.3 us
    pallas_call x1, Pallas kernels, local(): call(attend_kernel, shape((groups, chips, heads, KVL), BF16), [SMEM, SMEM...  10.3 us
    pallas_call x1, Pallas kernels, local(): call(prepare_kernel, (pltpu.VMEM((3, own, 128), F32), pltpu.VMEM(key_abso...  1.91 us
    pallas_call x1, Pallas kernels, local(): call(project_kernel, (pltpu.VMEM((own, width), F32), pltpu.VMEM((own, wid...  1.78 us
  transfers between devices with their start and end apart: 2, of which 1 were waited for; matrix products, arithmetic and copies ran while one was open for 0% of the time, Pallas kernels for 3%

profile of v2, /device:TPU:0, one launch (start us, length us, event | category | flops | bytes accessed | tf_op | source)
XLA Modules:
  0.0 74.2 jit_solution(435800619738282693)
XLA Ops:
  0.0 1.8 %project.1 = (f32[64,1536]{1,0:T(8,128)S(1)}, bf16[64,1536]{1,0:T(8,128)(2,1)S(1)}) custom-call(s32[1,128]{1,0:T(1,128)} %bitcast.12, bf16[192,128]{1,0:T(8,128)(2,1)} %bitcast.14, bf16[192,1536]{1,0:T(8,128)(2,1)} %query_up_hbm.1), custom_call_target="tpu_custom_call" | custom-call | tf_op jit(solution)/shard_map/project/pallas_call | solution.py:221
  1.8 0.1 collective-permute-start
  1.9 1.9 %prepare.1 = (f32[3,64,128]{2,1,0:T(8,128)S(1)}, bf16[8,128,512]{2,1,0:T(8,128)(2,1)S(1)}) custom-call(s32[128]{0:T(128)} %holder_ref.3, s32[128]{0:T(128)} %lengths_ref.3, f32[1,128]{1,0:T(1,128)} %constant.5.clone.frequency_ref, bf16[8,128,512]{2,1,0:T(8,128)(2,1)} %absorb_hbm.1), custom_call_target="tpu_custom_call" | custom-call | tf_op jit(solution)/shard_map/prepare/pallas_call | solution.py:234
  3.8 0.0 collective-permute-done.got_ref
  3.8 0.0 copy-start
  3.8 0.0 copy-start.1
  3.8 0.0 copy-start.4
  3.8 0.0 copy-start.5
  3.9 0.7 %absorb.1 = bf16[512,640]{1,0:T(8,128)(2,1)S(1)} custom-call(f32[64,1536]{1,0:T(8,128)S(1)} %get-tuple-element.9.mine_ref, bf16[64,1536]{1,0:T(8,128)(2,1)S(1)} %collective-permute-done.got_ref, f32[3,64,128]{2,1,0:T(8,128)S(1)} %get-tuple-element.11.angle_ref, bf16[8,128,512]{2,1,0:T(8,128)(2,1)S(1)} %get-tuple-element.12.absorb_ref, ...), custom_call_target="tpu_custom_call" | custom-call | tf_op jit(solution)/shard_map/absorb/pallas_call | solution.py:241
  4.6 26.7 %all_to_all.29 = bf16[64,8,640]{2,1,0:T(8,128)(2,1)S(1)} all-to-all(bf16[64,8,640]{2,1,0:T(8,128)(2,1)S(1)} %bitcast.8), channel_id=1, replica_groups=mesh['z'=4,'c'=2,'x'=4,'y'=4] {'x','y','z'}, dimensions={0} | all-to-all | bytes 1310720 | tf_op jit(solution)/shard_map/all_to_all | solution.py:202
  31.4 0.0 copy-done
  31.4 0.0 copy-done.1
  31.4 0.0 copy-done.4
  31.4 0.0 copy-done.5
  31.4 0.0 copy-start.3
  31.4 10.3 %attend.1 = bf16[16,4,8,512]{3,2,1,0:T(8,128)(2,1)S(1)} custom-call(s32[128]{0:T(128)S(1)} %copy-done.4, s32[128]{0:T(128)S(1)} %copy-done.5, bf16[16,4,8,640]{3,2,1,0:T(8,128)(2,1)S(1)} %bitcast.7, bf16[1,16384,512]{2,1,0:T(8,128)(2,1)S(1)} %copy-done, bf16[1,64,16384]{2,1,0:T(8,128)(2,1)S(1)} %copy-done.1), custom_call_target="tpu_custom_call" | custom-call | tf_op jit(solution)/shard_map/attend/pallas_call | solution.py:250
  41.6 0.0 copy-start.2
  41.7 17.0 %all_to_all.30 = bf16[64,8,512]{2,1,0:T(8,128)(2,1)S(1)} all-to-all(bf16[64,8,512]{2,1,0:T(8,128)(2,1)S(1)} %bitcast.9), channel_id=1, replica_groups=mesh['z'=4,'c'=2,'x'=4,'y'=4] {'x','y','z'}, dimensions={0} | all-to-all | bytes 1048576 | tf_op jit(solution)/shard_map/all_to_all | solution.py:202
  58.7 0.0 copy-done.3
  58.7 1.3 %values.1.own_ref = bf16[64,1024]{1,0:T(8,128)(2,1)S(1)} custom-call(bf16[512,512]{1,0:T(8,128)(2,1)S(1)} %bitcast.10, bf16[8,512,128]{2,1,0:T(8,128)(2,1)S(1)} %copy-done.3), custom_call_target="tpu_custom_call" | custom-call | tf_op jit(solution)/shard_map/values/pallas_call | solution.py:266
  60.0 0.1 collective-permute-start.1
  60.0 1.3 %collective-permute-done.1.pair_ref = bf16[64,1024]{1,0:T(8,128)(2,1)S(1)} collective-permute-done((bf16[64,1024]{1,0:T(8,128)(2,1)S(1)}, bf16[64,1024]{1,0:T(8,128)(2,1)S(1)}, u32[]{:S(2)}, u32[]{:S(2)}) %collective-permute-start.1) | collective-permute-done | bytes 131104 | tf_op jit(solution)/shard_map/ppermute | solution.py:198
  61.4 0.0 copy-done.2
  61.4 0.7 output.1
  62.1 11.5 %all_to_all.31 = bf16[16,8,896]{2,1,0:T(8,128)(2,1)S(1)} all-to-all(bf16[16,8,896]{2,1,0:T(8,128)(2,1)S(1)} %bitcast.11), channel_id=1, replica_groups=mesh['z'=4,'c'=2,'x'=4,'y'=4] {'x','y'}, dimensions={0} | all-to-all | bytes 458752 | tf_op jit(solution)/shard_map/all_to_all | solution.py:202
  73.6 0.6 reduce_sum.12
Async XLA Ops:
  1.8 2.0 %collective-permute-start = (bf16[64,1536]{1,0:T(8,128)(2,1)S(1)}, bf16[64,1536]{1,0:T(8,128)(2,1)S(1)}, u32[]{:S(2)}, u32[]{:S(2)}) collective-permute-start(bf16[64,1536]{1,0:T(8,128)(2,1)S(1)} %get-tuple-element.10), channel_id=1, source_target_pairs={{0,16},{16,0},{1,17},{17,1},{2,18},{18,2},{3,19},{19,3},{4,20},{20... | collective-permute-start | bytes 589832 | tf_op jit(solution)/shard_map/ppermute | solution.py:198
  3.8 27.5 %copy-start = (bf16[1,16384,512]{2,1,0:T(8,128)(2,1)S(1)}, bf16[1,16384,512]{2,1,0:T(8,128)(2,1)}, u32[]{:S(2)}) copy-start(bf16[1,16384,512]{2,1,0:T(8,128)(2,1)} %latent.1) | copy-start | bytes 50331652
  3.8 27.5 %copy-start.1 = (bf16[1,64,16384]{2,1,0:T(8,128)(2,1)S(1)}, bf16[1,64,16384]{2,1,0:T(8,128)(2,1)}, u32[]{:S(2)}) copy-start(bf16[1,64,16384]{2,1,0:T(8,128)(2,1)} %rope.1) | copy-start | bytes 6291460
  3.8 27.5 %copy-start.4 = (s32[128]{0:T(128)S(1)}, s32[128]{0:T(128)}, u32[]{:S(2)}) copy-start(s32[128]{0:T(128)} %holder_ref.3) | copy-start | bytes 1540
  3.8 27.5 %copy-start.5 = (s32[128]{0:T(128)S(1)}, s32[128]{0:T(128)}, u32[]{:S(2)}) copy-start(s32[128]{0:T(128)} %lengths_ref.3) | copy-start | bytes 1540
  31.4 27.3 %copy-start.3 = (bf16[8,512,128]{2,1,0:T(8,128)(2,1)S(1)}, bf16[8,512,128]{2,1,0:T(8,128)(2,1)}, u32[]{:S(2)}) copy-start(bf16[8,512,128]{2,1,0:T(8,128)(2,1)} %value_up_ref.1) | copy-start | bytes 3145732
  41.6 19.7 %copy-start.2 = (bf16[1024,896]{1,0:T(8,128)(2,1)S(1)}, bf16[1024,896]{1,0:T(8,128)(2,1)}, u32[]{:S(2)}) copy-start(bf16[1024,896]{1,0:T(8,128)(2,1)} %proj_ref.1) | copy-start | bytes 5505028
  60.0 1.4 %collective-permute-start.1 = (bf16[64,1024]{1,0:T(8,128)(2,1)S(1)}, bf16[64,1024]{1,0:T(8,128)(2,1)S(1)}, u32[]{:S(2)}, u32[]{:S(2)}) collective-permute-start(bf16[64,1024]{1,0:T(8,128)(2,1)S(1)} %values.1.own_ref), channel_id=1, source_target_pairs={{0,16},{16,0},{1,17},{17,1},{2,18},{18,2},{3,19},{19,3},{4,20},{20... | collective-permute-start | bytes 393224 | tf_op jit(solution)/shard_map/ppermute | solution.py:198

commit v3 on v2

--- a/solution.py
+++ b/solution.py
@@ -15,7 +15,7 @@
 HEAD = NOPE + ROPE
 VH = 128
 WIDE = 640
-CHUNK = 4096
+CHUNK = 8192
 PARTS = 4
 VMEM = pl.BlockSpec(memory_space=pltpu.VMEM)
 SMEM = pl.BlockSpec(memory_space=pltpu.SMEM)
@@ -36,62 +36,76 @@
     return (requests == holder_row).astype(F32).astype(BF16)
 
 
-def order_matrix(holder_row):
-    count = holder_row.shape[1]
+def place_matrix(count):
     row = lax.broadcasted_iota(jnp.int32, (count, count), 1)
     core = (row >> 6) ^ lax.axis_index("c")
     slot = ((row & 3) * 2 + core) * 16 + ((row >> 2) & 15)
     slots = lax.broadcasted_iota(jnp.int32, (count, count), 0)
-    place = (slots == slot).astype(F32).astype(BF16)
-    return dot(holder_matrix(holder_row), place).astype(BF16)
+    return (slots == slot).astype(F32).astype(BF16)
+
+
+def order_matrix(holder_row):
+    return dot(holder_matrix(holder_row), place_matrix(holder_row.shape[1])).astype(BF16)
 
 
 def project_kernel(
-    holder_hbm, compressed_hbm, query_up_hbm, mine_ref, other_ref, holder, compressed, query_up, sems
+    holder_hbm,
+    lengths_hbm,
+    frequency_hbm,
+    compressed_hbm,
+    query_up_hbm,
+    absorb_hbm,
+    mine_ref,
+    other_ref,
+    angle_ref,
+    absorb_ref,
+    holder,
+    lengths,
+    frequency,
+    compressed,
+    query_up,
+    sems,
 ):
     half, width = mine_ref.shape
     part = width // PARTS
-    copies = [
-        pltpu.make_async_copy(holder_hbm, holder, sems.at[0]),
-        pltpu.make_async_copy(compressed_hbm, compressed, sems.at[1]),
+    pairs = [
+        (holder_hbm, holder),
+        (lengths_hbm, lengths),
+        (frequency_hbm, frequency),
+        (compressed_hbm, compressed),
     ]
     for i in range(PARTS):
         at = pl.ds(i * part, part)
-        copies.append(
-            pltpu.make_async_copy(query_up_hbm.at[:, at], query_up.at[:, at], sems.at[2 + i])
-        )
+        pairs.append((query_up_hbm.at[:, at], query_up.at[:, at]))
+    pairs.append((absorb_hbm, absorb_ref))
+    copies = [
+        pltpu.make_async_copy(source, target, sems.at[i]) for i, (source, target) in enumerate(pairs)
+    ]
     for copy in copies:
         copy.start()
-    copies[0].wait()
-    order = order_matrix(holder[...])
-    copies[1].wait()
-    by_slot = dot(compressed[...], order).astype(BF16)
-    for i in range(PARTS):
-        at = slice(i * part, i * part + part)
-        copies[2 + i].wait()
-        term = dot(by_slot, query_up[:, at], 0, 0)
-        mine_ref[:, at] = term[:half]
-        other_ref[:, at] = term[half:].astype(BF16)
-
-
-def prepare_kernel(
-    holder_ref, lengths_ref, frequency_ref, absorb_hbm, angle_ref, absorb_ref, place_ref, sem
-):
-    copy = pltpu.make_async_copy(absorb_hbm, absorb_ref, sem)
-    copy.start()
-    core = lax.axis_index("c")
-    for j in range(place_ref.shape[0]):
-        slot = ((j & 3) * 2 + core) * 16 + (j >> 2)
-        place = (lengths_ref[holder_ref[slot]] - 1).astype(F32)
-        place_ref[j : j + 1, :] = jnp.full((1, 128), place, F32)
-    angles = place_ref[...] * frequency_ref[...]
+    for copy in copies[:3]:
+        copy.wait()
+    held = holder_matrix(holder[...])
+    place = place_matrix(held.shape[0])
+    order = dot(held, place).astype(BF16)
+    turned = dot(place, held, 0, 1)[:half]
+    last = jnp.sum(turned * (lengths[...] - 1).astype(F32), axis=1, keepdims=True)
+    angles = last * frequency[...]
     sin = jnp.sin(angles)
     lane = lax.broadcasted_iota(jnp.int32, angles.shape, 1)
     former = (lane & (ROPE - 1)) < ROPE // 2
     angle_ref[0] = jnp.cos(angles)
     angle_ref[1] = jnp.where(former, -sin, 0.0)
     angle_ref[2] = jnp.where(former, 0.0, sin)
-    copy.wait()
+    copies[3].wait()
+    by_slot = dot(compressed[...], order).astype(BF16)
+    for i in range(PARTS):
+        at = slice(i * part, i * part + part)
+        copies[4 + i].wait()
+        term = dot(by_slot, query_up[:, at], 0, 0)
+        mine_ref[:, at] = term[:half]
+        other_ref[:, at] = term[half:].astype(BF16)
+    copies[-1].wait()
 
 
 def absorb_kernel(
@@ -119,7 +133,7 @@
     out_ref[...] = wide_ref[...].reshape(out_ref.shape).astype(BF16)
 
 
-def attend_kernel(holder_ref, lengths_ref, query_ref, latent, rope, out_ref, scores):
+def attend_kernel(holder_ref, lengths_ref, query_ref, latent, rope, out_ref, scores, acc):
     slot = (lax.axis_index("z") * 2 + lax.axis_index("c")) * 16
     slot += lax.axis_index("x") * 4 + lax.axis_index("y")
     length = lengths_ref[holder_ref[slot]]
@@ -133,26 +147,28 @@
     query = query.reshape(count, WIDE) * (math.log2(math.e) / math.sqrt(HEAD))
     query_lat = query[:, :KVL].astype(BF16)
     query_rope = (query[:, KVL : KVL + ROPE] + query[:, KVL + ROPE :]).astype(BF16)
-    tops = []
-    for start in range(0, places, CHUNK):
-        at = slice(start, start + CHUNK)
+
+    def score(i, top):
+        start = pl.multiple_of(i * CHUNK, CHUNK)
+        at = pl.ds(start, CHUNK)
         s = dot(latent[0, at, :], query_lat, 1, 1) + dot(rope[0, :, at], query_rope, 0, 1)
         position = start + lax.broadcasted_iota(jnp.int32, s.shape, 0)
         s = jnp.where(position < length, s, -1e30)
         scores[at, :] = s
-        tops.append(jnp.max(s, axis=0, keepdims=True))
-    top = tops[0]
-    for other in tops[1:]:
-        top = jnp.maximum(top, other)
-    total = jnp.zeros((1, count), F32)
-    acc = jnp.zeros((count, KVL), F32)
-    for start in range(0, places, CHUNK):
-        at = slice(start, start + CHUNK)
+        return jnp.maximum(top, jnp.max(s, axis=0, keepdims=True))
+
+    top = lax.fori_loop(0, places // CHUNK, score, jnp.full((1, count), -1e30, F32))
+    acc[...] = jnp.zeros(acc.shape, F32)
+
+    def gather(i, total):
+        at = pl.ds(pl.multiple_of(i * CHUNK, CHUNK), CHUNK)
         p = jnp.exp2(scores[at, :] - top)
-        total += jnp.sum(p, axis=0, keepdims=True)
-        acc += dot(p.astype(BF16), latent[0, at, :], 0, 0)
+        acc[...] += dot(p.astype(BF16), latent[0, at, :], 0, 0)
+        return total + jnp.sum(p, axis=0, keepdims=True)
+
+    total = lax.fori_loop(0, places // CHUNK, gather, jnp.zeros((1, count), F32))
     total = jnp.transpose(jnp.broadcast_to(total, (count, count)))[:, :1]
-    result = (acc / total).reshape(groups, heads, KVL).astype(BF16)
+    result = (acc[...] / total).reshape(groups, heads, KVL).astype(BF16)
     for z in range(chips):
         out_ref[:, z] = result
 
@@ -218,26 +234,33 @@
     frequency = (10000.0 ** (-2.0 * half / ROPE)).astype(np.float32)
     frequency = jnp.asarray(np.tile(frequency, 4)[None, :])
 
-    mine, other = call(
+    mine, other, angles, absorb_in = call(
         project_kernel,
-        (pltpu.VMEM((own, width), F32), pltpu.VMEM((own, width), BF16)),
-        [ANY] * 3,
+        (
+            pltpu.VMEM((own, width), F32),
+            pltpu.VMEM((own, width), BF16),
+            pltpu.VMEM((3, own, 128), F32),
+            pltpu.VMEM(key_absorb.shape, BF16),
+        ),
+        [ANY] * 6,
         [
             pltpu.VMEM((1, batch), jnp.int32),
+            pltpu.VMEM((1, batch), jnp.int32),
+            pltpu.VMEM((1, 128), F32),
             pltpu.VMEM((compressed.shape[1], batch), BF16),
             pltpu.VMEM(query_up.shape, BF16),
-            pltpu.SemaphoreType.DMA((2 + PARTS,)),
+            pltpu.SemaphoreType.DMA((5 + PARTS,)),
         ],
         name="project",
-    )(stay(holder_row), stay(compressed.T), stay(query_up))
+    )(
+        stay(holder_row),
+        stay(lengths.reshape(1, batch)),
+        stay(frequency),
+        stay(compressed.T),
+        stay(query_up),
+        stay(key_absorb),
+    )
     got = swap_cores(other)
-    angles, absorb_in = call(
-        prepare_kernel,
-        (pltpu.VMEM((3, own, 128), F32), pltpu.VMEM(key_absorb.shape, BF16)),
-        [SMEM, SMEM, VMEM, ANY],
-        [pltpu.VMEM((own, 128), F32), pltpu.SemaphoreType.DMA],
-        name="prepare",
-    )(stay(holder), stay(lengths), stay(frequency), stay(key_absorb))
     queries = call(
         absorb_kernel,
         shape((own * heads, WIDE), BF16),
@@ -251,7 +274,7 @@
         attend_kernel,
         shape((groups, chips, heads, KVL), BF16),
         [SMEM, SMEM, VMEM, VMEM, VMEM],
-        [pltpu.VMEM((places, 128), F32)],
+        [pltpu.VMEM((places, 128), F32), pltpu.VMEM((128, KVL), F32)],
         limit=20,
         name="attend",
     )(

time: 74.5 us -> 72.5 us (0.973)
  Pallas kernels: 16.7 us -> 14.1 us
  waiting for transfers between devices: 1.34 us -> 2.76 us
  blocking collectives: 55.3 us -> 54.5 us
    pallas_call x1 -> x0, Pallas kernels: 1.91 us -> none  [local(): call(prepare_kernel, (pltpu.VMEM((3, own, 128), F32), pltpu.VMEM(key_abso...]
    ppermute x2, waiting for transfers between devices: 1.34 us -> 2.76 us  [swap_cores(): return lax.ppermute(array, 'c', [(0, 1), (1, 0)])]
    pallas_call x1, Pallas kernels: 10.3 us -> 9.3 us  [local(): call(attend_kernel, shape((groups, chips, heads, KVL), BF16), [SMEM, SMEM...]
  transfers between devices with their start and end apart: 2 -> 2, of which waited for: 1 -> 2; matrix products, arithmetic and copies ran while one was open for 0% -> 0% of each run, Pallas kernels for 3% -> 0%
where the time goes in v3:
time: 72.5 us; the launch traced here: 72.3 us
  blocking collectives  54.5 us (75%)
  Pallas kernels  14.1 us (19%)
  waiting for transfers between devices  2.76 us (4%)
    all_to_all x3, blocking collectives, exchange(): return lax.all_to_all(array, axes, split_axis=0, concat_axis=0, tiled=True)  54.5 us
    pallas_call x1, Pallas kernels, local(): call(attend_kernel, shape((groups, chips, heads, KVL), BF16), [SMEM, SMEM...  9.3 us
    ppermute x2, waiting for transfers between devices, swap_cores(): return lax.ppermute(array, 'c', [(0, 1), (1, 0)])  2.76 us
    pallas_call x1, Pallas kernels, local(): call(project_kernel, (pltpu.VMEM((own, width), F32), pltpu.VMEM((own, wid...  2.08 us
  transfers between devices with their start and end apart: 2, of which 2 were waited for; matrix products, arithmetic and copies ran while one was open for 0% of the time, Pallas kernels for 0%

profile of v3, /device:TPU:0, one launch (start us, length us, event | category | flops | bytes accessed | tf_op | source)
XLA Modules:
  0.0 72.3 jit_solution(10678898713499219611)
XLA Ops:
  0.0 2.1 %project.1 = (f32[64,1536]{1,0:T(8,128)S(1)}, bf16[64,1536]{1,0:T(8,128)(2,1)S(1)}, f32[3,64,128]{2,1,0:T(8,128)S(1)}, bf16[8,128,512]{2,1,0:T(8,128)(2,1)S(1)}) custom-call(s32[1,128]{1,0:T(1,128)} %bitcast.13, s32[1,128]{1,0:T(1,128)} %bitcast.15, f32[1,128]{1,0:T(1,128)} %constant.5.clone.frequency_hbm, bf16[192,128]{1,0:T(8,128)(2,1)} %bitcast.16, ...), custom_call_target="tpu_custom_call" | custom-call | tf_op jit(solution)/shard_map/project/pallas_call | solution.py:237
  2.1 0.1 collective-permute-start
  2.2 1.4 %collective-permute-done.got_ref = bf16[64,1536]{1,0:T(8,128)(2,1)S(1)} collective-permute-done((bf16[64,1536]{1,0:T(8,128)(2,1)S(1)}, bf16[64,1536]{1,0:T(8,128)(2,1)S(1)}, u32[]{:S(2)}, u32[]{:S(2)}) %collective-permute-start) | collective-permute-done | bytes 196640 | tf_op jit(solution)/shard_map/ppermute | solution.py:214
  3.6 0.0 copy-start
  3.6 0.0 copy-start.1
  3.6 0.0 copy-start.4
  3.6 0.0 copy-start.5
  3.6 0.7 %absorb.1 = bf16[512,640]{1,0:T(8,128)(2,1)S(1)} custom-call(f32[64,1536]{1,0:T(8,128)S(1)} %get-tuple-element.9.mine_ref, bf16[64,1536]{1,0:T(8,128)(2,1)S(1)} %collective-permute-done.got_ref, f32[3,64,128]{2,1,0:T(8,128)S(1)} %get-tuple-element.11.angle_ref, bf16[8,128,512]{2,1,0:T(8,128)(2,1)S(1)} %get-tuple-element.12.absorb_ref, ...), custom_call_target="tpu_custom_call" | custom-call | tf_op jit(solution)/shard_map/absorb/pallas_call | solution.py:264
  4.4 26.4 %all_to_all.29 = bf16[64,8,640]{2,1,0:T(8,128)(2,1)S(1)} all-to-all(bf16[64,8,640]{2,1,0:T(8,128)(2,1)S(1)} %bitcast.9), channel_id=1, replica_groups=mesh['z'=4,'c'=2,'x'=4,'y'=4] {'x','y','z'}, dimensions={0} | all-to-all | bytes 1310720 | tf_op jit(solution)/shard_map/all_to_all | solution.py:218
  30.8 0.0 copy-done
  30.8 0.0 copy-done.1
  30.8 0.0 copy-done.4
  30.8 0.0 copy-done.5
  30.8 0.0 copy-start.3
  30.8 9.3 %attend.1 = bf16[16,4,8,512]{3,2,1,0:T(8,128)(2,1)S(1)} custom-call(s32[128]{0:T(128)S(1)} %copy-done.4, s32[128]{0:T(128)S(1)} %copy-done.5, bf16[16,4,8,640]{3,2,1,0:T(8,128)(2,1)S(1)} %bitcast.8, bf16[1,16384,512]{2,1,0:T(8,128)(2,1)S(1)} %copy-done, bf16[1,64,16384]{2,1,0:T(8,128)(2,1)S(1)} %copy-done.1), custom_call_target="tpu_custom_call" | custom-call | tf_op jit(solution)/shard_map/attend/pallas_call | solution.py:273
  40.1 0.0 copy-start.2
  40.1 16.6 %all_to_all.30 = bf16[64,8,512]{2,1,0:T(8,128)(2,1)S(1)} all-to-all(bf16[64,8,512]{2,1,0:T(8,128)(2,1)S(1)} %bitcast.10), channel_id=1, replica_groups=mesh['z'=4,'c'=2,'x'=4,'y'=4] {'x','y','z'}, dimensions={0} | all-to-all | bytes 1048576 | tf_op jit(solution)/shard_map/all_to_all | solution.py:218
  56.7 0.0 copy-done.3
  56.7 1.3 %values.1.own_ref = bf16[64,1024]{1,0:T(8,128)(2,1)S(1)} custom-call(bf16[512,512]{1,0:T(8,128)(2,1)S(1)} %bitcast.11, bf16[8,512,128]{2,1,0:T(8,128)(2,1)S(1)} %copy-done.3), custom_call_target="tpu_custom_call" | custom-call | tf_op jit(solution)/shard_map/values/pallas_call | solution.py:289
  58.0 0.1 collective-permute-start.1
  58.1 1.3 %collective-permute-done.1.pair_ref = bf16[64,1024]{1,0:T(8,128)(2,1)S(1)} collective-permute-done((bf16[64,1024]{1,0:T(8,128)(2,1)S(1)}, bf16[64,1024]{1,0:T(8,128)(2,1)S(1)}, u32[]{:S(2)}, u32[]{:S(2)}) %collective-permute-start.1) | collective-permute-done | bytes 131104 | tf_op jit(solution)/shard_map/ppermute | solution.py:214
  59.4 0.0 copy-done.2
  59.4 0.7 output.1
  60.1 11.5 %all_to_all.31 = bf16[16,8,896]{2,1,0:T(8,128)(2,1)S(1)} all-to-all(bf16[16,8,896]{2,1,0:T(8,128)(2,1)S(1)} %bitcast.12), channel_id=1, replica_groups=mesh['z'=4,'c'=2,'x'=4,'y'=4] {'x','y'}, dimensions={0} | all-to-all | bytes 458752 | tf_op jit(solution)/shard_map/all_to_all | solution.py:218
  71.6 0.6 reduce_sum.12
Async XLA Ops:
  2.1 1.5 %collective-permute-start = (bf16[64,1536]{1,0:T(8,128)(2,1)S(1)}, bf16[64,1536]{1,0:T(8,128)(2,1)S(1)}, u32[]{:S(2)}, u32[]{:S(2)}) collective-permute-start(bf16[64,1536]{1,0:T(8,128)(2,1)S(1)} %get-tuple-element.10), channel_id=1, source_target_pairs={{0,16},{16,0},{1,17},{17,1},{2,18},{18,2},{3,19},{19,3},{4,20},{20... | collective-permute-start | bytes 589832 | tf_op jit(solution)/shard_map/ppermute | solution.py:214
  3.6 27.1 %copy-start = (bf16[1,16384,512]{2,1,0:T(8,128)(2,1)S(1)}, bf16[1,16384,512]{2,1,0:T(8,128)(2,1)}, u32[]{:S(2)}) copy-start(bf16[1,16384,512]{2,1,0:T(8,128)(2,1)} %latent.1) | copy-start | bytes 50331652
  3.6 27.1 %copy-start.1 = (bf16[1,64,16384]{2,1,0:T(8,128)(2,1)S(1)}, bf16[1,64,16384]{2,1,0:T(8,128)(2,1)}, u32[]{:S(2)}) copy-start(bf16[1,64,16384]{2,1,0:T(8,128)(2,1)} %rope.1) | copy-start | bytes 6291460
  3.6 27.1 %copy-start.4 = (s32[128]{0:T(128)S(1)}, s32[128]{0:T(128)}, u32[]{:S(2)}) copy-start(s32[128]{0:T(128)} %holder_ref.1) | copy-start | bytes 1540
  3.6 27.2 %copy-start.5 = (s32[128]{0:T(128)S(1)}, s32[128]{0:T(128)}, u32[]{:S(2)}) copy-start(s32[128]{0:T(128)} %lengths_ref.1) | copy-start | bytes 1540
  30.8 26.0 %copy-start.3 = (bf16[8,512,128]{2,1,0:T(8,128)(2,1)S(1)}, bf16[8,512,128]{2,1,0:T(8,128)(2,1)}, u32[]{:S(2)}) copy-start(bf16[8,512,128]{2,1,0:T(8,128)(2,1)} %value_up_ref.1) | copy-start | bytes 3145732
  40.1 19.3 %copy-start.2 = (bf16[1024,896]{1,0:T(8,128)(2,1)S(1)}, bf16[1024,896]{1,0:T(8,128)(2,1)}, u32[]{:S(2)}) copy-start(bf16[1024,896]{1,0:T(8,128)(2,1)} %proj_ref.1) | copy-start | bytes 5505028
  58.0 1.4 %collective-permute-start.1 = (bf16[64,1024]{1,0:T(8,128)(2,1)S(1)}, bf16[64,1024]{1,0:T(8,128)(2,1)S(1)}, u32[]{:S(2)}, u32[]{:S(2)}) collective-permute-start(bf16[64,1024]{1,0:T(8,128)(2,1)S(1)} %values.1.own_ref), channel_id=1, source_target_pairs={{0,16},{16,0},{1,17},{17,1},{2,18},{18,2},{3,19},{19,3},{4,20},{20... | collective-permute-start | bytes 393224 | tf_op jit(solution)/shard_map/ppermute | solution.py:214

commit v4 on v3

--- a/solution.py
+++ b/solution.py
@@ -15,8 +15,9 @@
 HEAD = NOPE + ROPE
 VH = 128
 WIDE = 640
-CHUNK = 8192
-PARTS = 4
+SCORED = 8192
+GATHERED = 16384
+PARTS = 1
 VMEM = pl.BlockSpec(memory_space=pltpu.VMEM)
 SMEM = pl.BlockSpec(memory_space=pltpu.SMEM)
 ANY = pl.BlockSpec(memory_space=pl.ANY)
@@ -42,10 +43,6 @@
     slot = ((row & 3) * 2 + core) * 16 + ((row >> 2) & 15)
     slots = lax.broadcasted_iota(jnp.int32, (count, count), 0)
     return (slots == slot).astype(F32).astype(BF16)
-
-
-def order_matrix(holder_row):
-    return dot(holder_matrix(holder_row), place_matrix(holder_row.shape[1])).astype(BF16)
 
 
 def project_kernel(
@@ -58,6 +55,7 @@
     mine_ref,
     other_ref,
     angle_ref,
+    order_ref,
     absorb_ref,
     holder,
     lengths,
@@ -87,18 +85,12 @@
         copy.wait()
     held = holder_matrix(holder[...])
     place = place_matrix(held.shape[0])
-    order = dot(held, place).astype(BF16)
+    order_ref[...] = dot(held, place).astype(BF16)
     turned = dot(place, held, 0, 1)[:half]
     last = jnp.sum(turned * (lengths[...] - 1).astype(F32), axis=1, keepdims=True)
-    angles = last * frequency[...]
-    sin = jnp.sin(angles)
-    lane = lax.broadcasted_iota(jnp.int32, angles.shape, 1)
-    former = (lane & (ROPE - 1)) < ROPE // 2
-    angle_ref[0] = jnp.cos(angles)
-    angle_ref[1] = jnp.where(former, -sin, 0.0)
-    angle_ref[2] = jnp.where(former, 0.0, sin)
+    angle_ref[...] = last * frequency[...]
     copies[3].wait()
-    by_slot = dot(compressed[...], order).astype(BF16)
+    by_slot = dot(compressed[...], order_ref[...]).astype(BF16)
     for i in range(PARTS):
         at = slice(i * part, i * part + part)
         copies[4 + i].wait()
@@ -106,6 +98,16 @@
         mine_ref[:, at] = term[:half]
         other_ref[:, at] = term[half:].astype(BF16)
     copies[-1].wait()
+
+
+def angle_kernel(angle_ref, out_ref):
+    angles = angle_ref[...]
+    sin = jnp.sin(angles)
+    lane = lax.broadcasted_iota(jnp.int32, angles.shape, 1)
+    former = (lane & (ROPE - 1)) < ROPE // 2
+    out_ref[0] = jnp.cos(angles)
+    out_ref[1] = jnp.where(former, -sin, 0.0)
+    out_ref[2] = jnp.where(former, 0.0, sin)
 
 
 def absorb_kernel(
@@ -149,42 +151,47 @@
     query_rope = (query[:, KVL : KVL + ROPE] + query[:, KVL + ROPE :]).astype(BF16)
 
     def score(i, top):
-        start = pl.multiple_of(i * CHUNK, CHUNK)
-        at = pl.ds(start, CHUNK)
+        start = pl.multiple_of(i * SCORED, SCORED)
+        at = pl.ds(start, SCORED)
         s = dot(latent[0, at, :], query_lat, 1, 1) + dot(rope[0, :, at], query_rope, 0, 1)
         position = start + lax.broadcasted_iota(jnp.int32, s.shape, 0)
         s = jnp.where(position < length, s, -1e30)
         scores[at, :] = s
         return jnp.maximum(top, jnp.max(s, axis=0, keepdims=True))
 
-    top = lax.fori_loop(0, places // CHUNK, score, jnp.full((1, count), -1e30, F32))
+    top = lax.fori_loop(0, places // SCORED, score, jnp.full((1, count), -1e30, F32))
     acc[...] = jnp.zeros(acc.shape, F32)
 
     def gather(i, total):
-        at = pl.ds(pl.multiple_of(i * CHUNK, CHUNK), CHUNK)
+        at = pl.ds(pl.multiple_of(i * GATHERED, GATHERED), GATHERED)
         p = jnp.exp2(scores[at, :] - top)
         acc[...] += dot(p.astype(BF16), latent[0, at, :], 0, 0)
         return total + jnp.sum(p, axis=0, keepdims=True)
 
-    total = lax.fori_loop(0, places // CHUNK, gather, jnp.zeros((1, count), F32))
+    total = lax.fori_loop(0, places // GATHERED, gather, jnp.zeros((1, count), F32))
     total = jnp.transpose(jnp.broadcast_to(total, (count, count)))[:, :1]
     result = (acc[...] / total).reshape(groups, heads, KVL).astype(BF16)
     for z in range(chips):
         out_ref[:, z] = result
 
 
-def value_kernel(latent_ref, value_up_ref, out_ref, wide_ref):
+def value_kernel(latent_ref, value_up_ref, out_ref):
     heads = value_up_ref.shape[0]
-    wide_ref[...] = latent_ref[...].astype(F32).reshape(wide_ref.shape)
+    rows = latent_ref.shape[0]
+    slots = rows // heads
+    row = lax.broadcasted_iota(jnp.int32, (rows, rows), 0)
+    came = lax.broadcasted_iota(jnp.int32, (rows, rows), 1)
+    by_head = ((row % slots) * heads + row // slots == came).astype(F32).astype(BF16)
+    latents = dot(by_head, latent_ref[...]).astype(BF16)
     for h in range(heads):
         out_ref[:, h * VH : h * VH + VH] = dot(
-            wide_ref[:, h, :].astype(BF16), value_up_ref[h]
+            latents[h * slots : h * slots + slots], value_up_ref[h]
         ).astype(BF16)
 
 
-def output_kernel(holder_ref, own_ref, pair_ref, proj_ref, out_ref):
+def output_kernel(order_ref, own_ref, pair_ref, proj_ref, out_ref):
     values = jnp.concatenate([own_ref[...], pair_ref[...]], axis=0)
-    values = dot(order_matrix(holder_ref[...]), values).astype(BF16)
+    values = dot(order_ref[...], values).astype(BF16)
     out_ref[...] = dot(values, proj_ref[...]).astype(BF16)
 
 
@@ -234,12 +241,13 @@
     frequency = (10000.0 ** (-2.0 * half / ROPE)).astype(np.float32)
     frequency = jnp.asarray(np.tile(frequency, 4)[None, :])
 
-    mine, other, angles, absorb_in = call(
+    mine, other, angles, order, absorb_in = call(
         project_kernel,
         (
             pltpu.VMEM((own, width), F32),
             pltpu.VMEM((own, width), BF16),
-            pltpu.VMEM((3, own, 128), F32),
+            pltpu.VMEM((own, 128), F32),
+            pltpu.VMEM((batch, batch), BF16),
             pltpu.VMEM(key_absorb.shape, BF16),
         ),
         [ANY] * 6,
@@ -261,6 +269,7 @@
         stay(key_absorb),
     )
     got = swap_cores(other)
+    angles = call(angle_kernel, pltpu.VMEM((3, own, 128), F32), [VMEM], name="angles")(angles)
     queries = call(
         absorb_kernel,
         shape((own * heads, WIDE), BF16),
@@ -290,7 +299,6 @@
         value_kernel,
         shape((own, heads * VH), BF16),
         [VMEM] * 2,
-        [pltpu.VMEM((own, heads, KVL), F32)],
         name="values",
     )(returned, value_up)
     partial = call(
@@ -298,7 +306,7 @@
         shape((batch, out_proj.shape[1]), BF16),
         [VMEM] * 4,
         name="output",
-    )(holder_row, values, swap_cores(values), out_proj)
+    )(order, values, swap_cores(values), out_proj)
     partial = exchange(partial, ("x", "y"))
     partial = partial.reshape(groups, batch // groups, out_proj.shape[1])
     return jnp.sum(partial.astype(F32), axis=0).astype(BF16)

time: 72.5 us -> 70.9 us (0.978)
  Pallas kernels: 14.1 us -> 12.6 us
where the time goes in v4:
time: 70.9 us; the launch traced here: 70.6 us
  blocking collectives  54.5 us (77%)
  Pallas kernels  12.6 us (18%)
  waiting for transfers between devices  2.63 us (4%)
    all_to_all x3, blocking collectives, exchange(): return lax.all_to_all(array, axes, split_axis=0, concat_axis=0, tiled=True)  54.5 us
    pallas_call x1, Pallas kernels, local(): call(attend_kernel, shape((groups, chips, heads, KVL), BF16), [SMEM, SMEM...  8.99 us
    ppermute x2, waiting for transfers between devices, swap_cores(): return lax.ppermute(array, 'c', [(0, 1), (1, 0)])  2.63 us
    pallas_call x1, Pallas kernels, local(): call(project_kernel, (pltpu.VMEM((own, width), F32), pltpu.VMEM((own, wid...  1.53 us
  transfers between devices with their start and end apart: 2, of which 2 were waited for; matrix products, arithmetic and copies ran while one was open for 0% of the time, Pallas kernels for 0%

profile of v4, /device:TPU:0, one launch (start us, length us, event | category | flops | bytes accessed | tf_op | source)
XLA Modules:
  0.0 70.6 jit_solution(6759168769702933903)
XLA Ops:
  0.0 1.5 %project.1 = (f32[64,1536]{1,0:T(8,128)S(1)}, bf16[64,1536]{1,0:T(8,128)(2,1)S(1)}, f32[64,128]{1,0:T(8,128)S(1)}, bf16[128,128]{1,0:T(8,128)(2,1)S(1)}, bf16[8,128,512]{2,1,0:T(8,128)(2,1)S(1)}) custom-call(s32[1,128]{1,0:T(1,128)} %bitcast.13, s32[1,128]{1,0:T(1,128)} %bitcast.14, f32[1,128]{1,0:T(1,128)} %constant.5.clone.frequency_hbm, ...), custom_call_target="tpu_custom_call" | custom-call | tf_op jit(solution)/shard_map/project/pallas_call | solution.py:244
  1.5 0.1 collective-permute-start
  1.6 0.1 angles.1.angle_ref
  1.8 1.3 %collective-permute-done.got_ref = bf16[64,1536]{1,0:T(8,128)(2,1)S(1)} collective-permute-done((bf16[64,1536]{1,0:T(8,128)(2,1)S(1)}, bf16[64,1536]{1,0:T(8,128)(2,1)S(1)}, u32[]{:S(2)}, u32[]{:S(2)}) %collective-permute-start) | collective-permute-done | bytes 196640 | tf_op jit(solution)/shard_map/ppermute | solution.py:221
  3.1 0.0 copy-start
  3.1 0.0 copy-start.1
  3.1 0.0 copy-start.4
  3.1 0.0 copy-start.5
  3.1 0.7 %absorb.1 = bf16[512,640]{1,0:T(8,128)(2,1)S(1)} custom-call(f32[64,1536]{1,0:T(8,128)S(1)} %get-tuple-element.11.mine_ref, bf16[64,1536]{1,0:T(8,128)(2,1)S(1)} %collective-permute-done.got_ref, f32[3,64,128]{2,1,0:T(8,128)S(1)} %angles.1.angle_ref, bf16[8,128,512]{2,1,0:T(8,128)(2,1)S(1)} %get-tuple-element.14.absorb_ref, bf16[1,16384,512]{2,1,0:T(8,128)(2,1)} %latent.1, ...), custom_call_target="tpu_custom_call" | custom-call | tf_op jit(solution)/shard_map/absorb/pallas_call | solution.py:273
  3.8 26.4 %all_to_all.29 = bf16[64,8,640]{2,1,0:T(8,128)(2,1)S(1)} all-to-all(bf16[64,8,640]{2,1,0:T(8,128)(2,1)S(1)} %bitcast.9), channel_id=1, replica_groups=mesh['z'=4,'c'=2,'x'=4,'y'=4] {'x','y','z'}, dimensions={0} | all-to-all | bytes 1310720 | tf_op jit(solution)/shard_map/all_to_all | solution.py:225
  30.2 0.0 copy-done
  30.2 0.0 copy-done.1
  30.2 0.0 copy-done.4
  30.2 0.0 copy-done.5
  30.2 0.0 copy-start.3
  30.2 9.0 %attend.1 = bf16[16,4,8,512]{3,2,1,0:T(8,128)(2,1)S(1)} custom-call(s32[128]{0:T(128)S(1)} %copy-done.4, s32[128]{0:T(128)S(1)} %copy-done.5, bf16[16,4,8,640]{3,2,1,0:T(8,128)(2,1)S(1)} %bitcast.8, bf16[1,16384,512]{2,1,0:T(8,128)(2,1)S(1)} %copy-done, bf16[1,64,16384]{2,1,0:T(8,128)(2,1)S(1)} %copy-done.1), custom_call_target="tpu_custom_call" | custom-call | tf_op jit(solution)/shard_map/attend/pallas_call | solution.py:282
  39.2 0.0 copy-start.2
  39.3 16.6 %all_to_all.30 = bf16[64,8,512]{2,1,0:T(8,128)(2,1)S(1)} all-to-all(bf16[64,8,512]{2,1,0:T(8,128)(2,1)S(1)} %bitcast.10), channel_id=1, replica_groups=mesh['z'=4,'c'=2,'x'=4,'y'=4] {'x','y','z'}, dimensions={0} | all-to-all | bytes 1048576 | tf_op jit(solution)/shard_map/all_to_all | solution.py:225
  55.9 0.0 copy-done.3
  55.9 0.6 values.1.own_ref
  56.5 0.1 collective-permute-start.1
  56.6 1.3 %collective-permute-done.1.pair_ref = bf16[64,1024]{1,0:T(8,128)(2,1)S(1)} collective-permute-done((bf16[64,1024]{1,0:T(8,128)(2,1)S(1)}, bf16[64,1024]{1,0:T(8,128)(2,1)S(1)}, u32[]{:S(2)}, u32[]{:S(2)}) %collective-permute-start.1) | collective-permute-done | bytes 131104 | tf_op jit(solution)/shard_map/ppermute | solution.py:221
  57.9 0.0 copy-done.2
  57.9 0.6 output.1
  58.5 11.5 %all_to_all.31 = bf16[16,8,896]{2,1,0:T(8,128)(2,1)S(1)} all-to-all(bf16[16,8,896]{2,1,0:T(8,128)(2,1)S(1)} %bitcast.12), channel_id=1, replica_groups=mesh['z'=4,'c'=2,'x'=4,'y'=4] {'x','y'}, dimensions={0} | all-to-all | bytes 458752 | tf_op jit(solution)/shard_map/all_to_all | solution.py:225
  70.0 0.6 reduce_sum.12
Async XLA Ops:
  1.5 1.5 %collective-permute-start = (bf16[64,1536]{1,0:T(8,128)(2,1)S(1)}, bf16[64,1536]{1,0:T(8,128)(2,1)S(1)}, u32[]{:S(2)}, u32[]{:S(2)}) collective-permute-start(bf16[64,1536]{1,0:T(8,128)(2,1)S(1)} %get-tuple-element.12), channel_id=1, source_target_pairs={{0,16},{16,0},{1,17},{17,1},{2,18},{18,2},{3,19},{19,3},{4,20},{20... | collective-permute-start | bytes 589832 | tf_op jit(solution)/shard_map/ppermute | solution.py:221
  3.1 27.1 %copy-start = (bf16[1,16384,512]{2,1,0:T(8,128)(2,1)S(1)}, bf16[1,16384,512]{2,1,0:T(8,128)(2,1)}, u32[]{:S(2)}) copy-start(bf16[1,16384,512]{2,1,0:T(8,128)(2,1)} %latent.1) | copy-start | bytes 50331652
  3.1 27.1 %copy-start.1 = (bf16[1,64,16384]{2,1,0:T(8,128)(2,1)S(1)}, bf16[1,64,16384]{2,1,0:T(8,128)(2,1)}, u32[]{:S(2)}) copy-start(bf16[1,64,16384]{2,1,0:T(8,128)(2,1)} %rope.1) | copy-start | bytes 6291460
  3.1 27.1 %copy-start.4 = (s32[128]{0:T(128)S(1)}, s32[128]{0:T(128)}, u32[]{:S(2)}) copy-start(s32[128]{0:T(128)} %holder_ref.1) | copy-start | bytes 1540
  3.1 27.2 %copy-start.5 = (s32[128]{0:T(128)S(1)}, s32[128]{0:T(128)}, u32[]{:S(2)}) copy-start(s32[128]{0:T(128)} %lengths_ref.1) | copy-start | bytes 1540
  30.2 25.7 %copy-start.3 = (bf16[8,512,128]{2,1,0:T(8,128)(2,1)S(1)}, bf16[8,512,128]{2,1,0:T(8,128)(2,1)}, u32[]{:S(2)}) copy-start(bf16[8,512,128]{2,1,0:T(8,128)(2,1)} %value_up_ref.1) | copy-start | bytes 3145732
  39.2 18.7 %copy-start.2 = (bf16[1024,896]{1,0:T(8,128)(2,1)S(1)}, bf16[1024,896]{1,0:T(8,128)(2,1)}, u32[]{:S(2)}) copy-start(bf16[1024,896]{1,0:T(8,128)(2,1)} %proj_ref.1) | copy-start | bytes 5505028
  56.5 1.4 %collective-permute-start.1 = (bf16[64,1024]{1,0:T(8,128)(2,1)S(1)}, bf16[64,1024]{1,0:T(8,128)(2,1)S(1)}, u32[]{:S(2)}, u32[]{:S(2)}) collective-permute-start(bf16[64,1024]{1,0:T(8,128)(2,1)S(1)} %values.1.own_ref), channel_id=1, source_target_pairs={{0,16},{16,0},{1,17},{17,1},{2,18},{18,2},{3,19},{19,3},{4,20},{20... | collective-permute-start | bytes 393224 | tf_op jit(solution)/shard_map/ppermute | solution.py:221

commit v5 on v4

--- a/solution.py
+++ b/solution.py
@@ -37,10 +37,14 @@
     return (requests == holder_row).astype(F32).astype(BF16)
 
 
-def place_matrix(count):
+def place_matrix(count, sending):
     row = lax.broadcasted_iota(jnp.int32, (count, count), 1)
     core = (row >> 6) ^ lax.axis_index("c")
-    slot = ((row & 3) * 2 + core) * 16 + ((row >> 2) & 15)
+    if sending:
+        chip, group = ((row >> 4) & 3) ^ lax.axis_index("z"), row & 15
+    else:
+        chip, group = row & 3, (row >> 2) & 15
+    slot = (chip * 2 + core) * 16 + group
     slots = lax.broadcasted_iota(jnp.int32, (count, count), 0)
     return (slots == slot).astype(F32).astype(BF16)
 
@@ -55,7 +59,7 @@
     mine_ref,
     other_ref,
     angle_ref,
-    order_ref,
+    held_ref,
     absorb_ref,
     holder,
     lengths,
@@ -84,13 +88,14 @@
     for copy in copies[:3]:
         copy.wait()
     held = holder_matrix(holder[...])
-    place = place_matrix(held.shape[0])
-    order_ref[...] = dot(held, place).astype(BF16)
-    turned = dot(place, held, 0, 1)[:half]
+    held_ref[...] = held
+    place = place_matrix(held.shape[0], True)
+    order = dot(held, place).astype(BF16)
+    turned = dot(place, held, 0, 1)[: angle_ref.shape[0]]
     last = jnp.sum(turned * (lengths[...] - 1).astype(F32), axis=1, keepdims=True)
     angle_ref[...] = last * frequency[...]
     copies[3].wait()
-    by_slot = dot(compressed[...], order_ref[...]).astype(BF16)
+    by_slot = dot(compressed[...], order).astype(BF16)
     for i in range(PARTS):
         at = slice(i * part, i * part + part)
         copies[4 + i].wait()
@@ -100,7 +105,7 @@
     copies[-1].wait()
 
 
-def angle_kernel(angle_ref, out_ref):
+def angle_kernel(angle_ref, held_ref, latent_hbm, rope_hbm, out_ref, order_ref):
     angles = angle_ref[...]
     sin = jnp.sin(angles)
     lane = lax.broadcasted_iota(jnp.int32, angles.shape, 1)
@@ -108,12 +113,26 @@
     out_ref[0] = jnp.cos(angles)
     out_ref[1] = jnp.where(former, -sin, 0.0)
     out_ref[2] = jnp.where(former, 0.0, sin)
+    held = held_ref[...]
+    order_ref[...] = dot(held, place_matrix(held.shape[0], False)).astype(BF16)
+
+
+def pair_kernel(mine_ref, got_ref, own_ref, one_ref, two_ref, three_ref):
+    rows = own_ref.shape[0]
+    for k, out_ref in enumerate((own_ref, one_ref, two_ref, three_ref)):
+        at = slice(k * rows, k * rows + rows)
+        out_ref[...] = (mine_ref[at] + got_ref[at].astype(F32)).astype(out_ref.dtype)
 
 
 def absorb_kernel(
-    mine_ref, got_ref, angle_ref, absorb_ref, latent_hbm, rope_hbm, out_ref, wide_ref
+    own_ref, one_ref, two_ref, three_ref, angle_ref, absorb_ref, out_ref, wide_ref
 ):
-    queries = mine_ref[...] + got_ref[...].astype(F32)
+    queries = (
+        own_ref[...]
+        + one_ref[...].astype(F32)
+        + two_ref[...].astype(F32)
+        + three_ref[...].astype(F32)
+    )
     lane = lax.broadcasted_iota(jnp.int32, (queries.shape[0], 128), 1)
     low = lane < 64
     for h in range(0, absorb_ref.shape[0], 2):
@@ -143,10 +162,7 @@
     groups, chips, heads = out_ref.shape[:3]
     count = groups * heads
 
-    query = query_ref[:, 0].astype(F32)
-    for z in range(1, chips):
-        query += query_ref[:, z].astype(F32)
-    query = query.reshape(count, WIDE) * (math.log2(math.e) / math.sqrt(HEAD))
+    query = query_ref[...].astype(F32) * (math.log2(math.e) / math.sqrt(HEAD))
     query_lat = query[:, :KVL].astype(BF16)
     query_rope = (query[:, KVL : KVL + ROPE] + query[:, KVL + ROPE :]).astype(BF16)
 
@@ -219,6 +235,10 @@
 
 def swap_cores(array):
     return lax.ppermute(array, "c", [(0, 1), (1, 0)])
+
+
+def swap_chips(array, distance):
+    return lax.ppermute(array, "z", [(i, i ^ distance) for i in range(lax.axis_size("z"))])
 
 
 def exchange(array, axes):
@@ -241,12 +261,12 @@
     frequency = (10000.0 ** (-2.0 * half / ROPE)).astype(np.float32)
     frequency = jnp.asarray(np.tile(frequency, 4)[None, :])
 
-    mine, other, angles, order, absorb_in = call(
+    mine, other, angles, held, absorb_in = call(
         project_kernel,
         (
             pltpu.VMEM((own, width), F32),
             pltpu.VMEM((own, width), BF16),
-            pltpu.VMEM((own, 128), F32),
+            pltpu.VMEM((groups, 128), F32),
             pltpu.VMEM((batch, batch), BF16),
             pltpu.VMEM(key_absorb.shape, BF16),
         ),
@@ -269,15 +289,28 @@
         stay(key_absorb),
     )
     got = swap_cores(other)
-    angles = call(angle_kernel, pltpu.VMEM((3, own, 128), F32), [VMEM], name="angles")(angles)
+    angles, order = call(
+        angle_kernel,
+        (pltpu.VMEM((3, groups, 128), F32), pltpu.VMEM((batch, batch), BF16)),
+        [VMEM] * 2 + [ANY] * 2,
+        name="angles",
+    )(angles, held, stay(cache_latent), stay(cache_rope))
+    part = shape((groups, width), BF16)
+    mine, one, two, three = call(
+        pair_kernel,
+        (shape((groups, width), F32), part, part, part),
+        [VMEM] * 2,
+        name="pair",
+    )(mine, got)
+    one, two, three = (swap_chips(array, k + 1) for k, array in enumerate((one, two, three)))
     queries = call(
         absorb_kernel,
-        shape((own * heads, WIDE), BF16),
-        [VMEM] * 4 + [ANY] * 2,
-        [pltpu.VMEM((own, heads, WIDE), F32)],
+        shape((groups * heads, WIDE), BF16),
+        [VMEM] * 6,
+        [pltpu.VMEM((groups, heads, WIDE), F32)],
         name="absorb",
-    )(mine, got, angles, absorb_in, stay(cache_latent), stay(cache_rope))
-    queries = exchange(queries, ("x", "y", "z"))
+    )(mine, one, two, three, angles, absorb_in)
+    queries = exchange(queries, ("x", "y"))
 
     latent_out = call(
         attend_kernel,
@@ -286,13 +319,7 @@
         [pltpu.VMEM((places, 128), F32), pltpu.VMEM((128, KVL), F32)],
         limit=20,
         name="attend",
-    )(
-        holder,
-        lengths,
-        queries.reshape(groups, chips, heads, WIDE),
-        keep(cache_latent),
-        keep(cache_rope),
-    )
+    )(holder, lengths, queries, keep(cache_latent), keep(cache_rope))
 
     returned = exchange(latent_out.reshape(own * heads, KVL), ("x", "y", "z"))
     values = call(

time: 70.9 us -> 69.4 us (0.979)
  blocking collectives: 54.5 us -> 42.5 us
  starting transfers between devices: 0.17 us -> 5.84 us
  waiting for transfers between devices: 2.63 us -> 7.87 us
    all_to_all x3, blocking collectives: 54.5 us -> 42.5 us  [exchange(): return lax.all_to_all(array, axes, split_axis=0, concat_axis=0, tiled=True)]
    ppermute x0 -> x3, starting transfers between devices: none -> 5.67 us  [swap_chips(): lax.ppermute(array, 'z', [(i, i ^ distance) for i in range(lax.axis_size(...]
    ppermute x0 -> x3, waiting for transfers between devices: none -> 5.11 us  [swap_chips(): lax.ppermute(array, 'z', [(i, i ^ distance) for i in range(lax.axis_size(...]
  transfers between devices with their start and end apart: 2 -> 5, of which waited for: 2 -> 4; matrix products, arithmetic and copies ran while one was open for 0% -> 0% of each run, Pallas kernels for 0% -> 0%
where the time goes in v5:
time: 69.4 us; the launch traced here: 69.1 us
  blocking collectives  42.5 us (61%)
  Pallas kernels  12.1 us (17%)
  waiting for transfers between devices  7.87 us (11%)
  starting transfers between devices  5.84 us (8%)
    all_to_all x3, blocking collectives, exchange(): return lax.all_to_all(array, axes, split_axis=0, concat_axis=0, tiled=True)  42.5 us
    pallas_call x1, Pallas kernels, local(): call(attend_kernel, shape((groups, chips, heads, KVL), BF16), [SMEM, SMEM...  8.95 us
    ppermute x3, starting transfers between devices, swap_chips(): lax.ppermute(array, 'z', [(i, i ^ distance) for i in range(lax.axis_size(...  5.67 us
    ppermute x3, waiting for transfers between devices, swap_chips(): lax.ppermute(array, 'z', [(i, i ^ distance) for i in range(lax.axis_size(...  5.11 us
    ppermute x2, waiting for transfers between devices, swap_cores(): return lax.ppermute(array, 'c', [(0, 1), (1, 0)])  2.76 us
    pallas_call x1, Pallas kernels, local(): call(project_kernel, (pltpu.VMEM((own, width), F32), pltpu.VMEM((own, wid...  1.53 us
  transfers between devices with their start and end apart: 5, of which 4 were waited for; matrix products, arithmetic and copies ran while one was open for 0% of the time, Pallas kernels for 0%

profile of v5, /device:TPU:0, one launch (start us, length us, event | category | flops | bytes accessed | tf_op | source)
XLA Modules:
  0.0 69.1 jit_solution(1806778339453114613)
XLA Ops:
  0.0 1.5 %project.1 = (f32[64,1536]{1,0:T(8,128)S(1)}, bf16[64,1536]{1,0:T(8,128)(2,1)S(1)}, f32[16,128]{1,0:T(8,128)S(1)}, bf16[128,128]{1,0:T(8,128)(2,1)S(1)}, bf16[8,128,512]{2,1,0:T(8,128)(2,1)S(1)}) custom-call(s32[1,128]{1,0:T(1,128)} %bitcast.13, s32[1,128]{1,0:T(1,128)} %bitcast.14, f32[1,128]{1,0:T(1,128)} %constant.5.clone.frequency_hbm, ...), custom_call_target="tpu_custom_call" | custom-call | tf_op jit(solution)/shard_map/project/pallas_call | solution.py:264
  1.5 0.1 collective-permute-start
  1.6 1.4 %collective-permute-done.got_ref = bf16[64,1536]{1,0:T(8,128)(2,1)S(1)} collective-permute-done((bf16[64,1536]{1,0:T(8,128)(2,1)S(1)}, bf16[64,1536]{1,0:T(8,128)(2,1)S(1)}, u32[]{:S(2)}, u32[]{:S(2)}) %collective-permute-start) | collective-permute-done | bytes 196640 | tf_op jit(solution)/shard_map/ppermute | solution.py:237
  3.1 2.1 %collective-permute-start.1 = (bf16[16,1536]{1,0:T(8,128)(2,1)S(1)}, bf16[16,1536]{1,0:T(8,128)(2,1)S(1)}, u32[]{:S(2)}, u32[]{:S(2)}) collective-permute-start(bf16[16,1536]{1,0:T(8,128)(2,1)S(1)} %get-tuple-element.22), channel_id=1, source_target_pairs={{0,32},{32,0},{64,96},{96,64},{1,33},{33,1},{65,97},{97,65},{2,34}... | collective-permute-start | bytes 147464 | tf_op jit(solution)/shard_map/ppermute | solution.py:241
  5.2 3.6 %collective-permute-start.2 = (bf16[16,1536]{1,0:T(8,128)(2,1)S(1)}, bf16[16,1536]{1,0:T(8,128)(2,1)S(1)}, u32[]{:S(2)}, u32[]{:S(2)}) collective-permute-start(bf16[16,1536]{1,0:T(8,128)(2,1)S(1)} %get-tuple-element.23), channel_id=1, source_target_pairs={{0,64},{32,96},{64,0},{96,32},{1,65},{33,97},{65,1},{97,33},{2,66}... | collective-permute-start | bytes 147464 | tf_op jit(solution)/shard_map/ppermute | solution.py:241
  8.8 0.0 collective-permute-start.3
  8.8 0.0 copy-start
  8.8 0.0 copy-start.1
  8.8 0.0 copy-start.4
  8.8 0.0 copy-start.5
  8.8 0.2 angles.1
  9.0 0.0 collective-permute-done.1.one_ref
  9.0 2.6 %collective-permute-done.2.two_ref = bf16[16,1536]{1,0:T(8,128)(2,1)S(1)} collective-permute-done((bf16[16,1536]{1,0:T(8,128)(2,1)S(1)}, bf16[16,1536]{1,0:T(8,128)(2,1)S(1)}, u32[]{:S(2)}, u32[]{:S(2)}) %collective-permute-start.2) | collective-permute-done | bytes 49184 | tf_op jit(solution)/shard_map/ppermute | solution.py:241
  11.6 2.5 %collective-permute-done.3.three_ref = bf16[16,1536]{1,0:T(8,128)(2,1)S(1)} collective-permute-done((bf16[16,1536]{1,0:T(8,128)(2,1)S(1)}, bf16[16,1536]{1,0:T(8,128)(2,1)S(1)}, u32[]{:S(2)}, u32[]{:S(2)}) %collective-permute-start.3) | collective-permute-done | bytes 49184 | tf_op jit(solution)/shard_map/ppermute | solution.py:241
  14.1 0.3 absorb.1
  14.4 14.8 %all_to_all.31 = bf16[16,8,640]{2,1,0:T(8,128)(2,1)S(1)} all-to-all(bf16[16,8,640]{2,1,0:T(8,128)(2,1)S(1)} %bitcast.12), channel_id=1, replica_groups=mesh['z'=4,'c'=2,'x'=4,'y'=4] {'x','y'}, dimensions={0} | all-to-all | bytes 327680 | tf_op jit(solution)/shard_map/all_to_all | solution.py:245
  29.2 0.0 copy-done
  29.2 0.0 copy-done.1
  29.2 0.0 copy-done.4
  29.2 0.0 copy-done.5
  29.2 0.0 copy-start.3
  29.2 8.9 %attend.1 = bf16[16,4,8,512]{3,2,1,0:T(8,128)(2,1)S(1)} custom-call(s32[128]{0:T(128)S(1)} %copy-done.4, s32[128]{0:T(128)S(1)} %copy-done.5, bf16[128,640]{1,0:T(8,128)(2,1)S(1)} %bitcast.11, bf16[1,16384,512]{2,1,0:T(8,128)(2,1)S(1)} %copy-done, bf16[1,64,16384]{2,1,0:T(8,128)(2,1)S(1)} %copy-done.1), custom_call_target="tpu_custom_call" | custom-call | tf_op jit(solution)/shard_map/attend/pallas_call | solution.py:315
  38.2 0.0 copy-start.2
  38.2 16.2 %all_to_all.32 = bf16[64,8,512]{2,1,0:T(8,128)(2,1)S(1)} all-to-all(bf16[64,8,512]{2,1,0:T(8,128)(2,1)S(1)} %bitcast.8), channel_id=1, replica_groups=mesh['z'=4,'c'=2,'x'=4,'y'=4] {'x','y','z'}, dimensions={0} | all-to-all | bytes 1048576 | tf_op jit(solution)/shard_map/all_to_all | solution.py:245
  54.4 0.0 copy-done.3
  54.4 0.6 values.1.own_ref
  55.0 0.1 collective-permute-start.4
  55.1 1.3 %collective-permute-done.4.pair_ref = bf16[64,1024]{1,0:T(8,128)(2,1)S(1)} collective-permute-done((bf16[64,1024]{1,0:T(8,128)(2,1)S(1)}, bf16[64,1024]{1,0:T(8,128)(2,1)S(1)}, u32[]{:S(2)}, u32[]{:S(2)}) %collective-permute-start.4) | collective-permute-done | bytes 131104 | tf_op jit(solution)/shard_map/ppermute | solution.py:237
  56.4 0.0 copy-done.2
  56.4 0.6 output.1
  57.0 11.5 %all_to_all.33 = bf16[16,8,896]{2,1,0:T(8,128)(2,1)S(1)} all-to-all(bf16[16,8,896]{2,1,0:T(8,128)(2,1)S(1)} %bitcast.10), channel_id=1, replica_groups=mesh['z'=4,'c'=2,'x'=4,'y'=4] {'x','y'}, dimensions={0} | all-to-all | bytes 458752 | tf_op jit(solution)/shard_map/all_to_all | solution.py:245
  68.5 0.6 reduce_sum.12
  (1 shorter events, 0.0 us)
Async XLA Ops:
  1.5 1.5 %collective-permute-start = (bf16[64,1536]{1,0:T(8,128)(2,1)S(1)}, bf16[64,1536]{1,0:T(8,128)(2,1)S(1)}, u32[]{:S(2)}, u32[]{:S(2)}) collective-permute-start(bf16[64,1536]{1,0:T(8,128)(2,1)S(1)} %get-tuple-element.20), channel_id=1, source_target_pairs={{0,16},{16,0},{1,17},{17,1},{2,18},{18,2},{3,19},{19,3},{4,20},{20... | collective-permute-start | bytes 589832 | tf_op jit(solution)/shard_map/ppermute | solution.py:237
  3.1 5.9 %collective-permute-start.1 = (bf16[16,1536]{1,0:T(8,128)(2,1)S(1)}, bf16[16,1536]{1,0:T(8,128)(2,1)S(1)}, u32[]{:S(2)}, u32[]{:S(2)}) collective-permute-start(bf16[16,1536]{1,0:T(8,128)(2,1)S(1)} %get-tuple-element.22), channel_id=1, source_target_pairs={{0,32},{32,0},{64,96},{96,64},{1,33},{33,1},{65,97},{97,65},{2,34}... | collective-permute-start | bytes 147464 | tf_op jit(solution)/shard_map/ppermute | solution.py:241
  5.2 6.4 %collective-permute-start.2 = (bf16[16,1536]{1,0:T(8,128)(2,1)S(1)}, bf16[16,1536]{1,0:T(8,128)(2,1)S(1)}, u32[]{:S(2)}, u32[]{:S(2)}) collective-permute-start(bf16[16,1536]{1,0:T(8,128)(2,1)S(1)} %get-tuple-element.23), channel_id=1, source_target_pairs={{0,64},{32,96},{64,0},{96,32},{1,65},{33,97},{65,1},{97,33},{2,66}... | collective-permute-start | bytes 147464 | tf_op jit(solution)/shard_map/ppermute | solution.py:241
  8.8 5.3 %collective-permute-start.3 = (bf16[16,1536]{1,0:T(8,128)(2,1)S(1)}, bf16[16,1536]{1,0:T(8,128)(2,1)S(1)}, u32[]{:S(2)}, u32[]{:S(2)}) collective-permute-start(bf16[16,1536]{1,0:T(8,128)(2,1)S(1)} %get-tuple-element.24), channel_id=1, source_target_pairs={{0,96},{32,64},{64,32},{96,0},{1,97},{33,65},{65,33},{97,1},{2,98}... | collective-permute-start | bytes 147464 | tf_op jit(solution)/shard_map/ppermute | solution.py:241
  8.8 20.4 %copy-start = (bf16[1,16384,512]{2,1,0:T(8,128)(2,1)S(1)}, bf16[1,16384,512]{2,1,0:T(8,128)(2,1)}, u32[]{:S(2)}) copy-start(bf16[1,16384,512]{2,1,0:T(8,128)(2,1)} %latent.1) | copy-start | bytes 50331652
  8.8 20.4 %copy-start.1 = (bf16[1,64,16384]{2,1,0:T(8,128)(2,1)S(1)}, bf16[1,64,16384]{2,1,0:T(8,128)(2,1)}, u32[]{:S(2)}) copy-start(bf16[1,64,16384]{2,1,0:T(8,128)(2,1)} %rope.1) | copy-start | bytes 6291460
  8.8 20.4 %copy-start.4 = (s32[128]{0:T(128)S(1)}, s32[128]{0:T(128)}, u32[]{:S(2)}) copy-start(s32[128]{0:T(128)} %holder_ref.1) | copy-start | bytes 1540
  8.8 20.4 %copy-start.5 = (s32[128]{0:T(128)S(1)}, s32[128]{0:T(128)}, u32[]{:S(2)}) copy-start(s32[128]{0:T(128)} %lengths_ref.1) | copy-start | bytes 1540
  29.2 25.2 %copy-start.3 = (bf16[8,512,128]{2,1,0:T(8,128)(2,1)S(1)}, bf16[8,512,128]{2,1,0:T(8,128)(2,1)}, u32[]{:S(2)}) copy-start(bf16[8,512,128]{2,1,0:T(8,128)(2,1)} %value_up_ref.1) | copy-start | bytes 3145732
  38.2 18.2 %copy-start.2 = (bf16[1024,896]{1,0:T(8,128)(2,1)S(1)}, bf16[1024,896]{1,0:T(8,128)(2,1)}, u32[]{:S(2)}) copy-start(bf16[1024,896]{1,0:T(8,128)(2,1)} %proj_ref.1) | copy-start | bytes 5505028
  55.0 1.4 %collective-permute-start.4 = (bf16[64,1024]{1,0:T(8,128)(2,1)S(1)}, bf16[64,1024]{1,0:T(8,128)(2,1)S(1)}, u32[]{:S(2)}, u32[]{:S(2)}) collective-permute-start(bf16[64,1024]{1,0:T(8,128)(2,1)S(1)} %values.1.own_ref), channel_id=1, source_target_pairs={{0,16},{16,0},{1,17},{17,1},{2,18},{18,2},{3,19},{19,3},{4,20},{20... | collective-permute-start | bytes 393224 | tf_op jit(solution)/shard_map/ppermute | solution.py:237

commit v6 on v5

--- a/solution.py
+++ b/solution.py
@@ -17,7 +17,7 @@
 WIDE = 640
 SCORED = 8192
 GATHERED = 16384
-PARTS = 1
+PARTS = 2
 VMEM = pl.BlockSpec(memory_space=pltpu.VMEM)
 SMEM = pl.BlockSpec(memory_space=pltpu.SMEM)
 ANY = pl.BlockSpec(memory_space=pl.ANY)
@@ -56,53 +56,47 @@
     compressed_hbm,
     query_up_hbm,
     absorb_hbm,
-    mine_ref,
     other_ref,
-    angle_ref,
     held_ref,
-    absorb_ref,
+    lengths_ref,
+    frequency_ref,
+    by_slot_ref,
+    query_up_ref,
     holder,
-    lengths,
-    frequency,
     compressed,
-    query_up,
     sems,
 ):
-    half, width = mine_ref.shape
-    part = width // PARTS
-    pairs = [
-        (holder_hbm, holder),
-        (lengths_hbm, lengths),
-        (frequency_hbm, frequency),
-        (compressed_hbm, compressed),
-    ]
+    half = other_ref.shape[0]
+    depth = query_up_ref.shape[0] // PARTS
+    pairs = [(holder_hbm, holder), (compressed_hbm, compressed)]
     for i in range(PARTS):
-        at = pl.ds(i * part, part)
-        pairs.append((query_up_hbm.at[:, at], query_up.at[:, at]))
-    pairs.append((absorb_hbm, absorb_ref))
+        at = pl.ds(i * depth, depth)
+        pairs.append((query_up_hbm.at[at, :], query_up_ref.at[at, :]))
+    pairs += [(lengths_hbm, lengths_ref), (frequency_hbm, frequency_ref)]
     copies = [
         pltpu.make_async_copy(source, target, sems.at[i]) for i, (source, target) in enumerate(pairs)
     ]
     for copy in copies:
         copy.start()
-    for copy in copies[:3]:
-        copy.wait()
+    copies[0].wait()
     held = holder_matrix(holder[...])
     held_ref[...] = held
+    order = dot(held, place_matrix(held.shape[0], True)).astype(BF16)
+    copies[1].wait()
+    by_slot = dot(compressed[...], order).astype(BF16)
+    by_slot_ref[...] = by_slot
+    for copy in copies[2:]:
+        copy.wait()
+    other_ref[...] = dot(by_slot[:, half:], query_up_ref[...], 0, 0).astype(BF16)
+
+
+def mine_kernel(by_slot_ref, query_up_ref, held_ref, lengths_ref, frequency_ref, mine_ref, angle_ref):
+    mine_ref[...] = dot(by_slot_ref[:, : mine_ref.shape[0]], query_up_ref[...], 0, 0)
+    held = held_ref[...]
     place = place_matrix(held.shape[0], True)
-    order = dot(held, place).astype(BF16)
     turned = dot(place, held, 0, 1)[: angle_ref.shape[0]]
-    last = jnp.sum(turned * (lengths[...] - 1).astype(F32), axis=1, keepdims=True)
-    angle_ref[...] = last * frequency[...]
-    copies[3].wait()
-    by_slot = dot(compressed[...], order).astype(BF16)
-    for i in range(PARTS):
-        at = slice(i * part, i * part + part)
-        copies[4 + i].wait()
-        term = dot(by_slot, query_up[:, at], 0, 0)
-        mine_ref[:, at] = term[:half]
-        other_ref[:, at] = term[half:].astype(BF16)
-    copies[-1].wait()
+    last = jnp.sum(turned * (lengths_ref[...] - 1).astype(F32), axis=1, keepdims=True)
+    angle_ref[...] = last * frequency_ref[...]
 
 
 def angle_kernel(angle_ref, held_ref, latent_hbm, rope_hbm, out_ref, order_ref):
@@ -125,7 +119,7 @@
 
 
 def absorb_kernel(
-    own_ref, one_ref, two_ref, three_ref, angle_ref, absorb_ref, out_ref, wide_ref
+    own_ref, two_ref, one_ref, three_ref, angle_ref, absorb_ref, out_ref, wide_ref
 ):
     queries = (
         own_ref[...]
@@ -261,23 +255,21 @@
     frequency = (10000.0 ** (-2.0 * half / ROPE)).astype(np.float32)
     frequency = jnp.asarray(np.tile(frequency, 4)[None, :])
 
-    mine, other, angles, held, absorb_in = call(
+    other, held, lengths_row, frequency, by_slot, weights = call(
         project_kernel,
         (
-            pltpu.VMEM((own, width), F32),
             pltpu.VMEM((own, width), BF16),
-            pltpu.VMEM((groups, 128), F32),
             pltpu.VMEM((batch, batch), BF16),
-            pltpu.VMEM(key_absorb.shape, BF16),
+            pltpu.VMEM((1, batch), jnp.int32),
+            pltpu.VMEM((1, 128), F32),
+            pltpu.VMEM((compressed.shape[1], batch), BF16),
+            pltpu.VMEM(query_up.shape, BF16),
         ),
         [ANY] * 6,
         [
             pltpu.VMEM((1, batch), jnp.int32),
-            pltpu.VMEM((1, batch), jnp.int32),
-            pltpu.VMEM((1, 128), F32),
             pltpu.VMEM((compressed.shape[1], batch), BF16),
-            pltpu.VMEM(query_up.shape, BF16),
-            pltpu.SemaphoreType.DMA((5 + PARTS,)),
+            pltpu.SemaphoreType.DMA((4 + PARTS,)),
         ],
         name="project",
     )(
@@ -289,6 +281,12 @@
         stay(key_absorb),
     )
     got = swap_cores(other)
+    mine, angles = call(
+        mine_kernel,
+        (pltpu.VMEM((own, width), F32), pltpu.VMEM((groups, 128), F32)),
+        [VMEM] * 5,
+        name="mine",
+    )(by_slot, weights, held, lengths_row, frequency)
     angles, order = call(
         angle_kernel,
         (pltpu.VMEM((3, groups, 128), F32), pltpu.VMEM((batch, batch), BF16)),
@@ -309,7 +307,7 @@
         [VMEM] * 6,
         [pltpu.VMEM((groups, heads, WIDE), F32)],
         name="absorb",
-    )(mine, one, two, three, angles, absorb_in)
+    )(mine, two, one, three, angles, keep(key_absorb))
     queries = exchange(queries, ("x", "y"))
 
     latent_out = call(

time: 69.4 us -> 68.7 us (0.990)
    pallas_call x1 -> x2, Pallas kernels: 1.53 us -> 1.8 us  [the longest x1 1.47 us: local(): call(project_kernel, (pltpu.VMEM((own, width), BF16), pltpu.VMEM((batch,...]
  transfers between devices with their start and end apart: 5 -> 5, of which waited for: 4 -> 5; matrix products, arithmetic and copies ran while one was open for 0% -> 0% of each run, Pallas kernels for 0% -> 1%
where the time goes in v6:
time: 68.7 us; the launch traced here: 68.5 us
  blocking collectives  42.5 us (62%)
  Pallas kernels  12.4 us (18%)
  waiting for transfers between devices  7.55 us (11%)
  starting transfers between devices  5.23 us (8%)
    all_to_all x3, blocking collectives, exchange(): return lax.all_to_all(array, axes, split_axis=0, concat_axis=0, tiled=True)  42.5 us
    pallas_call x1, Pallas kernels, local(): call(attend_kernel, shape((groups, chips, heads, KVL), BF16), [SMEM, SMEM...  8.94 us
    ppermute x3, waiting for transfers between devices, swap_chips(): lax.ppermute(array, 'z', [(i, i ^ distance) for i in range(lax.axis_size(...  5.11 us
    ppermute x3, starting transfers between devices, swap_chips(): lax.ppermute(array, 'z', [(i, i ^ distance) for i in range(lax.axis_size(...  5.06 us
    ppermute x2, waiting for transfers between devices, swap_cores(): return lax.ppermute(array, 'c', [(0, 1), (1, 0)])  2.44 us
    pallas_call x1, Pallas kernels, local(): call(project_kernel, (pltpu.VMEM((own, width), BF16), pltpu.VMEM((batch,...  1.47 us
  transfers between devices with their start and end apart: 5, of which 5 were waited for; matrix products, arithmetic and copies ran while one was open for 0% of the time, Pallas kernels for 1%

profile of v6, /device:TPU:0, one launch (start us, length us, event | category | flops | bytes accessed | tf_op | source)
XLA Modules:
  0.0 68.5 jit_solution(1981916389486026917)
XLA Ops:
  0.0 1.5 %project.1 = (bf16[64,1536]{1,0:T(8,128)(2,1)S(1)}, bf16[128,128]{1,0:T(8,128)(2,1)S(1)}, s32[1,128]{1,0:T(1,128)S(1)}, f32[1,128]{1,0:T(1,128)S(1)}, bf16[192,1...) custom-call(s32[1,128]{1,0:T(1,128)} %bitcast.13, s32[1,128]{1,0:T(1,128)} %bitcast.14, ...), custom_call_target="tpu_custom_call" | custom-call | tf_op jit(solution)/shard_map/project/pallas_call | solution.py:258
  1.5 0.1 collective-permute-start
  1.6 0.3 mine.1
  1.9 1.1 %collective-permute-done.got_ref = bf16[64,1536]{1,0:T(8,128)(2,1)S(1)} collective-permute-done((bf16[64,1536]{1,0:T(8,128)(2,1)S(1)}, bf16[64,1536]{1,0:T(8,128)(2,1)S(1)}, u32[]{:S(2)}, u32[]{:S(2)}) %collective-permute-start) | collective-permute-done | bytes 196640 | tf_op jit(solution)/shard_map/ppermute | solution.py:231
  3.0 0.1 pair.1
  3.1 4.0 %collective-permute-start.1 = (bf16[16,1536]{1,0:T(8,128)(2,1)S(1)}, bf16[16,1536]{1,0:T(8,128)(2,1)S(1)}, u32[]{:S(2)}, u32[]{:S(2)}) collective-permute-start(bf16[16,1536]{1,0:T(8,128)(2,1)S(1)} %get-tuple-element.29), channel_id=1, source_target_pairs={{0,64},{32,96},{64,0},{96,32},{1,65},{33,97},{65,1},{97,33},{2,66}... | collective-permute-start | bytes 147464 | tf_op jit(solution)/shard_map/ppermute | solution.py:235
  7.1 1.0 %collective-permute-start.2 = (bf16[16,1536]{1,0:T(8,128)(2,1)S(1)}, bf16[16,1536]{1,0:T(8,128)(2,1)S(1)}, u32[]{:S(2)}, u32[]{:S(2)}) collective-permute-start(bf16[16,1536]{1,0:T(8,128)(2,1)S(1)} %get-tuple-element.30), channel_id=1, source_target_pairs={{0,32},{32,0},{64,96},{96,64},{1,33},{33,1},{65,97},{97,65},{2,34}... | collective-permute-start | bytes 147464 | tf_op jit(solution)/shard_map/ppermute | solution.py:235
  8.1 0.0 collective-permute-start.3
  8.1 0.0 copy-start.6
  8.1 0.2 angles.1
  8.3 0.9 %collective-permute-done.1.two_ref = bf16[16,1536]{1,0:T(8,128)(2,1)S(1)} collective-permute-done((bf16[16,1536]{1,0:T(8,128)(2,1)S(1)}, bf16[16,1536]{1,0:T(8,128)(2,1)S(1)}, u32[]{:S(2)}, u32[]{:S(2)}) %collective-permute-start.1) | collective-permute-done | bytes 49184 | tf_op jit(solution)/shard_map/ppermute | solution.py:235
  9.2 2.0 %collective-permute-done.2.one_ref = bf16[16,1536]{1,0:T(8,128)(2,1)S(1)} collective-permute-done((bf16[16,1536]{1,0:T(8,128)(2,1)S(1)}, bf16[16,1536]{1,0:T(8,128)(2,1)S(1)}, u32[]{:S(2)}, u32[]{:S(2)}) %collective-permute-start.2) | collective-permute-done | bytes 49184 | tf_op jit(solution)/shard_map/ppermute | solution.py:235
  11.2 2.2 %collective-permute-done.3.three_ref = bf16[16,1536]{1,0:T(8,128)(2,1)S(1)} collective-permute-done((bf16[16,1536]{1,0:T(8,128)(2,1)S(1)}, bf16[16,1536]{1,0:T(8,128)(2,1)S(1)}, u32[]{:S(2)}, u32[]{:S(2)}) %collective-permute-start.3) | collective-permute-done | bytes 49184 | tf_op jit(solution)/shard_map/ppermute | solution.py:235
  13.4 0.0 copy-done.2
  13.4 0.3 absorb.1
  13.8 14.8 %all_to_all.31 = bf16[16,8,640]{2,1,0:T(8,128)(2,1)S(1)} all-to-all(bf16[16,8,640]{2,1,0:T(8,128)(2,1)S(1)} %bitcast.12), channel_id=1, replica_groups=mesh['z'=4,'c'=2,'x'=4,'y'=4] {'x','y'}, dimensions={0} | all-to-all | bytes 327680 | tf_op jit(solution)/shard_map/all_to_all | solution.py:239
  28.5 0.0 copy-done
  28.5 0.0 copy-done.1
  28.5 0.0 copy-done.5
  28.5 0.0 copy-done.6
  28.6 0.0 copy-start.4
  28.6 8.9 %attend.1 = bf16[16,4,8,512]{3,2,1,0:T(8,128)(2,1)S(1)} custom-call(s32[128]{0:T(128)S(1)} %copy-done.5, s32[128]{0:T(128)S(1)} %copy-done.6, bf16[128,640]{1,0:T(8,128)(2,1)S(1)} %bitcast.11, bf16[1,16384,512]{2,1,0:T(8,128)(2,1)S(1)} %copy-done, bf16[1,64,16384]{2,1,0:T(8,128)(2,1)S(1)} %copy-done.1), custom_call_target="tpu_custom_call" | custom-call | tf_op jit(solution)/shard_map/attend/pallas_call | solution.py:313
  37.5 0.0 copy-start.3
  37.5 16.2 %all_to_all.32 = bf16[64,8,512]{2,1,0:T(8,128)(2,1)S(1)} all-to-all(bf16[64,8,512]{2,1,0:T(8,128)(2,1)S(1)} %bitcast.8), channel_id=1, replica_groups=mesh['z'=4,'c'=2,'x'=4,'y'=4] {'x','y','z'}, dimensions={0} | all-to-all | bytes 1048576 | tf_op jit(solution)/shard_map/all_to_all | solution.py:239
  53.7 0.0 copy-done.4
  53.7 0.6 values.1.own_ref
  54.3 0.1 collective-permute-start.4
  54.4 1.3 %collective-permute-done.4.pair_ref = bf16[64,1024]{1,0:T(8,128)(2,1)S(1)} collective-permute-done((bf16[64,1024]{1,0:T(8,128)(2,1)S(1)}, bf16[64,1024]{1,0:T(8,128)(2,1)S(1)}, u32[]{:S(2)}, u32[]{:S(2)}) %collective-permute-start.4) | collective-permute-done | bytes 131104 | tf_op jit(solution)/shard_map/ppermute | solution.py:231
  55.8 0.0 copy-done.3
  55.8 0.6 output.1
  56.3 11.5 %all_to_all.33 = bf16[16,8,896]{2,1,0:T(8,128)(2,1)S(1)} all-to-all(bf16[16,8,896]{2,1,0:T(8,128)(2,1)S(1)} %bitcast.10), channel_id=1, replica_groups=mesh['z'=4,'c'=2,'x'=4,'y'=4] {'x','y'}, dimensions={0} | all-to-all | bytes 458752 | tf_op jit(solution)/shard_map/all_to_all | solution.py:239
  67.8 0.6 reduce_sum.12
  (4 shorter events, 0.0 us)
Async XLA Ops:
  1.5 1.5 %collective-permute-start = (bf16[64,1536]{1,0:T(8,128)(2,1)S(1)}, bf16[64,1536]{1,0:T(8,128)(2,1)S(1)}, u32[]{:S(2)}, u32[]{:S(2)}) collective-permute-start(bf16[64,1536]{1,0:T(8,128)(2,1)S(1)} %get-tuple-element.27), channel_id=1, source_target_pairs={{0,16},{16,0},{1,17},{17,1},{2,18},{18,2},{3,19},{19,3},{4,20},{20... | collective-permute-start | bytes 589832 | tf_op jit(solution)/shard_map/ppermute | solution.py:231
  3.0 10.4 %copy-start.2 = (bf16[8,128,512]{2,1,0:T(8,128)(2,1)S(1)}, bf16[8,128,512]{2,1,0:T(8,128)(2,1)}, u32[]{:S(2)}) copy-start(bf16[8,128,512]{2,1,0:T(8,128)(2,1)} %absorb_ref.1) | copy-start | bytes 3145732
  3.1 6.1 %collective-permute-start.1 = (bf16[16,1536]{1,0:T(8,128)(2,1)S(1)}, bf16[16,1536]{1,0:T(8,128)(2,1)S(1)}, u32[]{:S(2)}, u32[]{:S(2)}) collective-permute-start(bf16[16,1536]{1,0:T(8,128)(2,1)S(1)} %get-tuple-element.29), channel_id=1, source_target_pairs={{0,64},{32,96},{64,0},{96,32},{1,65},{33,97},{65,1},{97,33},{2,66}... | collective-permute-start | bytes 147464 | tf_op jit(solution)/shard_map/ppermute | solution.py:235
  7.1 4.1 %collective-permute-start.2 = (bf16[16,1536]{1,0:T(8,128)(2,1)S(1)}, bf16[16,1536]{1,0:T(8,128)(2,1)S(1)}, u32[]{:S(2)}, u32[]{:S(2)}) collective-permute-start(bf16[16,1536]{1,0:T(8,128)(2,1)S(1)} %get-tuple-element.30), channel_id=1, source_target_pairs={{0,32},{32,0},{64,96},{96,64},{1,33},{33,1},{65,97},{97,65},{2,34}... | collective-permute-start | bytes 147464 | tf_op jit(solution)/shard_map/ppermute | solution.py:235
  8.1 5.3 %collective-permute-start.3 = (bf16[16,1536]{1,0:T(8,128)(2,1)S(1)}, bf16[16,1536]{1,0:T(8,128)(2,1)S(1)}, u32[]{:S(2)}, u32[]{:S(2)}) collective-permute-start(bf16[16,1536]{1,0:T(8,128)(2,1)S(1)} %get-tuple-element.31), channel_id=1, source_target_pairs={{0,96},{32,64},{64,32},{96,0},{1,97},{33,65},{65,33},{97,1},{2,98}... | collective-permute-start | bytes 147464 | tf_op jit(solution)/shard_map/ppermute | solution.py:235
  8.1 20.4 %copy-start = (bf16[1,16384,512]{2,1,0:T(8,128)(2,1)S(1)}, bf16[1,16384,512]{2,1,0:T(8,128)(2,1)}, u32[]{:S(2)}) copy-start(bf16[1,16384,512]{2,1,0:T(8,128)(2,1)} %latent.1) | copy-start | bytes 50331652
  8.1 20.4 %copy-start.1 = (bf16[1,64,16384]{2,1,0:T(8,128)(2,1)S(1)}, bf16[1,64,16384]{2,1,0:T(8,128)(2,1)}, u32[]{:S(2)}) copy-start(bf16[1,64,16384]{2,1,0:T(8,128)(2,1)} %rope.1) | copy-start | bytes 6291460
  8.1 20.4 %copy-start.5 = (s32[128]{0:T(128)S(1)}, s32[128]{0:T(128)}, u32[]{:S(2)}) copy-start(s32[128]{0:T(128)} %holder_ref.1) | copy-start | bytes 1540
  8.1 20.4 %copy-start.6 = (s32[128]{0:T(128)S(1)}, s32[128]{0:T(128)}, u32[]{:S(2)}) copy-start(s32[128]{0:T(128)} %lengths_ref.1) | copy-start | bytes 1540
  28.6 25.2 %copy-start.4 = (bf16[8,512,128]{2,1,0:T(8,128)(2,1)S(1)}, bf16[8,512,128]{2,1,0:T(8,128)(2,1)}, u32[]{:S(2)}) copy-start(bf16[8,512,128]{2,1,0:T(8,128)(2,1)} %value_up_ref.1) | copy-start | bytes 3145732
  37.5 18.2 %copy-start.3 = (bf16[1024,896]{1,0:T(8,128)(2,1)S(1)}, bf16[1024,896]{1,0:T(8,128)(2,1)}, u32[]{:S(2)}) copy-start(bf16[1024,896]{1,0:T(8,128)(2,1)} %proj_ref.1) | copy-start | bytes 5505028
  54.3 1.4 %collective-permute-start.4 = (bf16[64,1024]{1,0:T(8,128)(2,1)S(1)}, bf16[64,1024]{1,0:T(8,128)(2,1)S(1)}, u32[]{:S(2)}, u32[]{:S(2)}) collective-permute-start(bf16[64,1024]{1,0:T(8,128)(2,1)S(1)} %values.1.own_ref), channel_id=1, source_target_pairs={{0,16},{16,0},{1,17},{17,1},{2,18},{18,2},{3,19},{19,3},{4,20},{20... | collective-permute-start | bytes 393224 | tf_op jit(solution)/shard_map/ppermute | solution.py:231

commit v7 on v6

--- a/solution.py
+++ b/solution.py
@@ -99,7 +99,7 @@
     angle_ref[...] = last * frequency_ref[...]
 
 
-def angle_kernel(angle_ref, held_ref, latent_hbm, rope_hbm, out_ref, order_ref):
+def angle_kernel(angle_ref, held_ref, latent_hbm, rope_hbm, out_ref, order_ref, regroup_ref):
     angles = angle_ref[...]
     sin = jnp.sin(angles)
     lane = lax.broadcasted_iota(jnp.int32, angles.shape, 1)
@@ -109,6 +109,11 @@
     out_ref[2] = jnp.where(former, 0.0, sin)
     held = held_ref[...]
     order_ref[...] = dot(held, place_matrix(held.shape[0], False)).astype(BF16)
+    rows, slots = regroup_ref.shape[0], held.shape[0] // 2
+    row = lax.broadcasted_iota(jnp.int32, (rows, rows), 0)
+    came = lax.broadcasted_iota(jnp.int32, (rows, rows), 1)
+    by_head = (row % slots) * (rows // slots) + row // slots == came
+    regroup_ref[...] = by_head.astype(F32).astype(BF16)
 
 
 def pair_kernel(mine_ref, got_ref, own_ref, one_ref, two_ref, three_ref):
@@ -185,14 +190,11 @@
         out_ref[:, z] = result
 
 
-def value_kernel(latent_ref, value_up_ref, out_ref):
+def value_kernel(regroup_ref, latent_ref, value_up_ref, out_ref):
     heads = value_up_ref.shape[0]
     rows = latent_ref.shape[0]
     slots = rows // heads
-    row = lax.broadcasted_iota(jnp.int32, (rows, rows), 0)
-    came = lax.broadcasted_iota(jnp.int32, (rows, rows), 1)
-    by_head = ((row % slots) * heads + row // slots == came).astype(F32).astype(BF16)
-    latents = dot(by_head, latent_ref[...]).astype(BF16)
+    latents = dot(regroup_ref[...], latent_ref[...]).astype(BF16)
     for h in range(heads):
         out_ref[:, h * VH : h * VH + VH] = dot(
             latents[h * slots : h * slots + slots], value_up_ref[h]
@@ -287,9 +289,13 @@
         [VMEM] * 5,
         name="mine",
     )(by_slot, weights, held, lengths_row, frequency)
-    angles, order = call(
+    angles, order, regroup = call(
         angle_kernel,
-        (pltpu.VMEM((3, groups, 128), F32), pltpu.VMEM((batch, batch), BF16)),
+        (
+            pltpu.VMEM((3, groups, 128), F32),
+            pltpu.VMEM((batch, batch), BF16),
+            pltpu.VMEM((own * heads, own * heads), BF16),
+        ),
         [VMEM] * 2 + [ANY] * 2,
         name="angles",
     )(angles, held, stay(cache_latent), stay(cache_rope))
@@ -323,9 +329,9 @@
     values = call(
         value_kernel,
         shape((own, heads * VH), BF16),
-        [VMEM] * 2,
+        [VMEM] * 3,
         name="values",
-    )(returned, value_up)
+    )(regroup, returned, value_up)
     partial = call(
         output_kernel,
         shape((batch, out_proj.shape[1]), BF16),

time: 68.7 us -> 68.7 us (level)
  no operation moved by 1% of the time
where the time goes in v7:
time: 68.7 us; the launch traced here: 68.5 us
  blocking collectives  42.5 us (62%)
  Pallas kernels  12.6 us (18%)
  waiting for transfers between devices  7.34 us (11%)
  starting transfers between devices  5.23 us (8%)
    all_to_all x3, blocking collectives, exchange(): return lax.all_to_all(array, axes, split_axis=0, concat_axis=0, tiled=True)  42.5 us
    pallas_call x1, Pallas kernels, local(): call(attend_kernel, shape((groups, chips, heads, KVL), BF16), [SMEM, SMEM...  8.94 us
    ppermute x3, starting transfers between devices, swap_chips(): lax.ppermute(array, 'z', [(i, i ^ distance) for i in range(lax.axis_size(...  5.06 us
    ppermute x3, waiting for transfers between devices, swap_chips(): lax.ppermute(array, 'z', [(i, i ^ distance) for i in range(lax.axis_size(...  4.9 us
    ppermute x2, waiting for transfers between devices, swap_cores(): return lax.ppermute(array, 'c', [(0, 1), (1, 0)])  2.44 us
    pallas_call x1, Pallas kernels, local(): call(project_kernel, (pltpu.VMEM((own, width), BF16), pltpu.VMEM((batch,...  1.47 us
  transfers between devices with their start and end apart: 5, of which 5 were waited for; matrix products, arithmetic and copies ran while one was open for 0% of the time, Pallas kernels for 1%

profile of v7, /device:TPU:0, one launch (start us, length us, event | category | flops | bytes accessed | tf_op | source)
XLA Modules:
  0.0 68.5 jit_solution(13070619993912960101)
XLA Ops:
  0.0 1.5 %project.1 = (bf16[64,1536]{1,0:T(8,128)(2,1)S(1)}, bf16[128,128]{1,0:T(8,128)(2,1)S(1)}, s32[1,128]{1,0:T(1,128)S(1)}, f32[1,128]{1,0:T(1,128)S(1)}, bf16[192,1...) custom-call(s32[1,128]{1,0:T(1,128)} %bitcast.13, s32[1,128]{1,0:T(1,128)} %bitcast.14, ...), custom_call_target="tpu_custom_call" | custom-call | tf_op jit(solution)/shard_map/project/pallas_call | solution.py:260
  1.5 0.1 collective-permute-start
  1.6 0.3 mine.1
  1.9 1.1 %collective-permute-done.got_ref = bf16[64,1536]{1,0:T(8,128)(2,1)S(1)} collective-permute-done((bf16[64,1536]{1,0:T(8,128)(2,1)S(1)}, bf16[64,1536]{1,0:T(8,128)(2,1)S(1)}, u32[]{:S(2)}, u32[]{:S(2)}) %collective-permute-start) | collective-permute-done | bytes 196640 | tf_op jit(solution)/shard_map/ppermute | solution.py:233
  3.0 0.1 pair.1
  3.1 4.0 %collective-permute-start.1 = (bf16[16,1536]{1,0:T(8,128)(2,1)S(1)}, bf16[16,1536]{1,0:T(8,128)(2,1)S(1)}, u32[]{:S(2)}, u32[]{:S(2)}) collective-permute-start(bf16[16,1536]{1,0:T(8,128)(2,1)S(1)} %get-tuple-element.31), channel_id=1, source_target_pairs={{0,64},{32,96},{64,0},{96,32},{1,65},{33,97},{65,1},{97,33},{2,66}... | collective-permute-start | bytes 147464 | tf_op jit(solution)/shard_map/ppermute | solution.py:237
  7.1 1.0 %collective-permute-start.2 = (bf16[16,1536]{1,0:T(8,128)(2,1)S(1)}, bf16[16,1536]{1,0:T(8,128)(2,1)S(1)}, u32[]{:S(2)}, u32[]{:S(2)}) collective-permute-start(bf16[16,1536]{1,0:T(8,128)(2,1)S(1)} %get-tuple-element.32), channel_id=1, source_target_pairs={{0,32},{32,0},{64,96},{96,64},{1,33},{33,1},{65,97},{97,65},{2,34}... | collective-permute-start | bytes 147464 | tf_op jit(solution)/shard_map/ppermute | solution.py:237
  8.1 0.0 collective-permute-start.3
  8.1 0.0 copy-start.6
  8.1 0.4 angles.1
  8.5 0.6 collective-permute-done.1.two_ref
  9.2 2.0 %collective-permute-done.2.one_ref = bf16[16,1536]{1,0:T(8,128)(2,1)S(1)} collective-permute-done((bf16[16,1536]{1,0:T(8,128)(2,1)S(1)}, bf16[16,1536]{1,0:T(8,128)(2,1)S(1)}, u32[]{:S(2)}, u32[]{:S(2)}) %collective-permute-start.2) | collective-permute-done | bytes 49184 | tf_op jit(solution)/shard_map/ppermute | solution.py:237
  11.2 2.2 %collective-permute-done.3.three_ref = bf16[16,1536]{1,0:T(8,128)(2,1)S(1)} collective-permute-done((bf16[16,1536]{1,0:T(8,128)(2,1)S(1)}, bf16[16,1536]{1,0:T(8,128)(2,1)S(1)}, u32[]{:S(2)}, u32[]{:S(2)}) %collective-permute-start.3) | collective-permute-done | bytes 49184 | tf_op jit(solution)/shard_map/ppermute | solution.py:237
  13.4 0.0 copy-done.2
  13.4 0.3 absorb.1
  13.8 14.8 %all_to_all.31 = bf16[16,8,640]{2,1,0:T(8,128)(2,1)S(1)} all-to-all(bf16[16,8,640]{2,1,0:T(8,128)(2,1)S(1)} %bitcast.12), channel_id=1, replica_groups=mesh['z'=4,'c'=2,'x'=4,'y'=4] {'x','y'}, dimensions={0} | all-to-all | bytes 327680 | tf_op jit(solution)/shard_map/all_to_all | solution.py:241
  28.5 0.0 copy-done
  28.5 0.0 copy-done.1
  28.5 0.0 copy-done.5
  28.5 0.0 copy-done.6
  28.6 0.0 copy-start.4
  28.6 8.9 %attend.1 = bf16[16,4,8,512]{3,2,1,0:T(8,128)(2,1)S(1)} custom-call(s32[128]{0:T(128)S(1)} %copy-done.5, s32[128]{0:T(128)S(1)} %copy-done.6, bf16[128,640]{1,0:T(8,128)(2,1)S(1)} %bitcast.11, bf16[1,16384,512]{2,1,0:T(8,128)(2,1)S(1)} %copy-done, bf16[1,64,16384]{2,1,0:T(8,128)(2,1)S(1)} %copy-done.1), custom_call_target="tpu_custom_call" | custom-call | tf_op jit(solution)/shard_map/attend/pallas_call | solution.py:319
  37.5 0.0 copy-start.3
  37.5 16.2 %all_to_all.32 = bf16[64,8,512]{2,1,0:T(8,128)(2,1)S(1)} all-to-all(bf16[64,8,512]{2,1,0:T(8,128)(2,1)S(1)} %bitcast.9), channel_id=1, replica_groups=mesh['z'=4,'c'=2,'x'=4,'y'=4] {'x','y','z'}, dimensions={0} | all-to-all | bytes 1048576 | tf_op jit(solution)/shard_map/all_to_all | solution.py:241
  53.7 0.0 copy-done.4
  53.7 0.6 values.1.own_ref
  54.3 0.1 collective-permute-start.4
  54.4 1.3 %collective-permute-done.4.pair_ref = bf16[64,1024]{1,0:T(8,128)(2,1)S(1)} collective-permute-done((bf16[64,1024]{1,0:T(8,128)(2,1)S(1)}, bf16[64,1024]{1,0:T(8,128)(2,1)S(1)}, u32[]{:S(2)}, u32[]{:S(2)}) %collective-permute-start.4) | collective-permute-done | bytes 131104 | tf_op jit(solution)/shard_map/ppermute | solution.py:233
  55.8 0.0 copy-done.3
  55.8 0.6 output.1
  56.3 11.5 %all_to_all.33 = bf16[16,8,896]{2,1,0:T(8,128)(2,1)S(1)} all-to-all(bf16[16,8,896]{2,1,0:T(8,128)(2,1)S(1)} %bitcast.10), channel_id=1, replica_groups=mesh['z'=4,'c'=2,'x'=4,'y'=4] {'x','y'}, dimensions={0} | all-to-all | bytes 458752 | tf_op jit(solution)/shard_map/all_to_all | solution.py:241
  67.8 0.6 reduce_sum.12
  (4 shorter events, 0.0 us)
Async XLA Ops:
  1.5 1.5 %collective-permute-start = (bf16[64,1536]{1,0:T(8,128)(2,1)S(1)}, bf16[64,1536]{1,0:T(8,128)(2,1)S(1)}, u32[]{:S(2)}, u32[]{:S(2)}) collective-permute-start(bf16[64,1536]{1,0:T(8,128)(2,1)S(1)} %get-tuple-element.29), channel_id=1, source_target_pairs={{0,16},{16,0},{1,17},{17,1},{2,18},{18,2},{3,19},{19,3},{4,20},{20... | collective-permute-start | bytes 589832 | tf_op jit(solution)/shard_map/ppermute | solution.py:233
  3.0 10.4 %copy-start.2 = (bf16[8,128,512]{2,1,0:T(8,128)(2,1)S(1)}, bf16[8,128,512]{2,1,0:T(8,128)(2,1)}, u32[]{:S(2)}) copy-start(bf16[8,128,512]{2,1,0:T(8,128)(2,1)} %absorb_ref.1) | copy-start | bytes 3145732
  3.1 6.1 %collective-permute-start.1 = (bf16[16,1536]{1,0:T(8,128)(2,1)S(1)}, bf16[16,1536]{1,0:T(8,128)(2,1)S(1)}, u32[]{:S(2)}, u32[]{:S(2)}) collective-permute-start(bf16[16,1536]{1,0:T(8,128)(2,1)S(1)} %get-tuple-element.31), channel_id=1, source_target_pairs={{0,64},{32,96},{64,0},{96,32},{1,65},{33,97},{65,1},{97,33},{2,66}... | collective-permute-start | bytes 147464 | tf_op jit(solution)/shard_map/ppermute | solution.py:237
  7.1 4.1 %collective-permute-start.2 = (bf16[16,1536]{1,0:T(8,128)(2,1)S(1)}, bf16[16,1536]{1,0:T(8,128)(2,1)S(1)}, u32[]{:S(2)}, u32[]{:S(2)}) collective-permute-start(bf16[16,1536]{1,0:T(8,128)(2,1)S(1)} %get-tuple-element.32), channel_id=1, source_target_pairs={{0,32},{32,0},{64,96},{96,64},{1,33},{33,1},{65,97},{97,65},{2,34}... | collective-permute-start | bytes 147464 | tf_op jit(solution)/shard_map/ppermute | solution.py:237
  8.1 5.3 %collective-permute-start.3 = (bf16[16,1536]{1,0:T(8,128)(2,1)S(1)}, bf16[16,1536]{1,0:T(8,128)(2,1)S(1)}, u32[]{:S(2)}, u32[]{:S(2)}) collective-permute-start(bf16[16,1536]{1,0:T(8,128)(2,1)S(1)} %get-tuple-element.33), channel_id=1, source_target_pairs={{0,96},{32,64},{64,32},{96,0},{1,97},{33,65},{65,33},{97,1},{2,98}... | collective-permute-start | bytes 147464 | tf_op jit(solution)/shard_map/ppermute | solution.py:237
  8.1 20.4 %copy-start = (bf16[1,16384,512]{2,1,0:T(8,128)(2,1)S(1)}, bf16[1,16384,512]{2,1,0:T(8,128)(2,1)}, u32[]{:S(2)}) copy-start(bf16[1,16384,512]{2,1,0:T(8,128)(2,1)} %latent.1) | copy-start | bytes 50331652
  8.1 20.4 %copy-start.1 = (bf16[1,64,16384]{2,1,0:T(8,128)(2,1)S(1)}, bf16[1,64,16384]{2,1,0:T(8,128)(2,1)}, u32[]{:S(2)}) copy-start(bf16[1,64,16384]{2,1,0:T(8,128)(2,1)} %rope.1) | copy-start | bytes 6291460
  8.1 20.4 %copy-start.5 = (s32[128]{0:T(128)S(1)}, s32[128]{0:T(128)}, u32[]{:S(2)}) copy-start(s32[128]{0:T(128)} %holder_ref.1) | copy-start | bytes 1540
  8.1 20.4 %copy-start.6 = (s32[128]{0:T(128)S(1)}, s32[128]{0:T(128)}, u32[]{:S(2)}) copy-start(s32[128]{0:T(128)} %lengths_ref.1) | copy-start | bytes 1540
  28.6 25.2 %copy-start.4 = (bf16[8,512,128]{2,1,0:T(8,128)(2,1)S(1)}, bf16[8,512,128]{2,1,0:T(8,128)(2,1)}, u32[]{:S(2)}) copy-start(bf16[8,512,128]{2,1,0:T(8,128)(2,1)} %value_up_ref.1) | copy-start | bytes 3145732
  37.5 18.2 %copy-start.3 = (bf16[1024,896]{1,0:T(8,128)(2,1)S(1)}, bf16[1024,896]{1,0:T(8,128)(2,1)}, u32[]{:S(2)}) copy-start(bf16[1024,896]{1,0:T(8,128)(2,1)} %proj_ref.1) | copy-start | bytes 5505028
  54.3 1.4 %collective-permute-start.4 = (bf16[64,1024]{1,0:T(8,128)(2,1)S(1)}, bf16[64,1024]{1,0:T(8,128)(2,1)S(1)}, u32[]{:S(2)}, u32[]{:S(2)}) collective-permute-start(bf16[64,1024]{1,0:T(8,128)(2,1)S(1)} %values.1.own_ref), channel_id=1, source_target_pairs={{0,16},{16,0},{1,17},{17,1},{2,18},{18,2},{3,19},{19,3},{4,20},{20... | collective-permute-start | bytes 393224 | tf_op jit(solution)/shard_map/ppermute | solution.py:233
